TPU v7x, 128 devices: a whole 4x4x4 slice. The times are simulated.
128 devices in a mesh: depth: 2 (over core), lat: 64 (over z, y, x).
Axes of the slice: x: 4, y: 4, z: 4, core: 2. Of those that a mesh axis runs over, the one named last changes fastest.
Arguments:
- transmission: float32 [2, 4, 4096, 1024], P(None, 'depth', 'lat')
- probe: float32 [2, 128, 128], replicated, may hold values from -6 to 6
- amplitude: float32 [256, 128, 128], P('lat'), may hold values from 0.2 to 3
- positions: int32 [256, 2], P('lat'), may hold values from 0 to 4095, as said below
- counts: int32 [64], P('lat'), may hold values from 1 to 4, as said below
Outputs:
- gradient: float32 [2, 4, 4096, 1024], P(None, 'depth', 'lat')
Inputs may be any that keep to these rules, and one draw needn't show every extreme that they name: positions[p][0] lies in the rows of tile p // 4, that is between (p // 4) * 64 and (p // 4 + 1) * 64 - 1; positions[p][1] is a column of the object; every slot, live or not, holds such a position. `counts`: the largest count is 4.
All inputs are finite; a program needn't handle non-finite values.
Results may differ from a plain program's by a relative error of at most 0.0003.
Values sent between devices are 32-bit elements; how exact they have to be, the bound alone decides.
A program may use at most 64 MiB of HBM per device.

v0:
```python
import math

import jax
import jax.numpy as jnp
from jax import lax
from jax.sharding import PartitionSpec as P

PROP_COEF = 40.0
HIGHEST = lax.Precision.HIGHEST


def padded_2(cells, sides, width):
    for axis, dim in sides:
        count = lax.axis_size(axis)
        ends = count - 1
        head = lax.slice_in_dim(cells, 0, width, axis=dim)
        tail = lax.slice_in_dim(cells, cells.shape[dim] - width, cells.shape[dim], axis=dim)
        cells = jnp.concatenate(
            [
                lax.ppermute(tail, axis, [(i, (i + 1) % count) for i in range(ends)]),
                cells,
                lax.ppermute(head, axis, [((i + 1) % count, i) for i in range(ends)]),
            ],
            axis=dim,
        )
    return cells


def from_behind(value, axis, steps):
    count = lax.axis_size(axis)
    leading, last = (max(0, -steps), min(count, count - steps))
    return lax.ppermute(value, axis, [(source, source + steps) for source in range(leading, last)])


def dft_tables(width):
    index = jnp.arange(width, dtype=jnp.int32)
    product = index[:, None] * index[None, :] % width
    angle = 2.0 * math.pi / width * product.astype(jnp.float32)
    scale = 1.0 / math.sqrt(width)
    return (jnp.cos(angle) * scale, -jnp.sin(angle) * scale)


def propagator(width):
    index = jnp.arange(width, dtype=jnp.int32)
    signed = (index + width // 2) % width - width // 2
    freq = signed.astype(jnp.float32) / width
    phase = -PROP_COEF * (freq[:, None] * freq[:, None] + freq[None, :] * freq[None, :])
    return (jnp.cos(phase), jnp.sin(phase))


def left_mul(table, values):
    return jnp.einsum("jk,pkl->pjl", table, values, precision=HIGHEST)


def right_mul(values, table):
    return jnp.einsum("pjk,kl->pjl", values, table, precision=HIGHEST)


def transform(real_part, imag_part, cosine, sine):
    first_re = left_mul(cosine, real_part) - left_mul(sine, imag_part)
    first_im = left_mul(cosine, imag_part) + left_mul(sine, real_part)
    out_re = right_mul(first_re, cosine) - right_mul(first_im, sine)
    out_im = right_mul(first_re, sine) + right_mul(first_im, cosine)
    return (out_re, out_im)


def on_device(transmission, probe, amplitude, positions, counts):
    width = probe.shape[-1]
    half = width // 2
    slabs = transmission.shape[1]
    strip = transmission.shape[2]
    columns = transmission.shape[3]
    slots = positions.shape[0]
    cosine, sine = dft_tables(width)
    prop_re, prop_im = propagator(width)

    def propagate(real_part, imag_part):
        freq_re, freq_im = transform(real_part, imag_part, cosine, sine)
        moved_re = freq_re * prop_re - freq_im * prop_im
        moved_im = freq_re * prop_im + freq_im * prop_re
        return transform(moved_re, moved_im, cosine, -sine)

    def back_propagate(real_part, imag_part):
        freq_re, freq_im = transform(real_part, imag_part, cosine, sine)
        moved_re = freq_re * prop_re + freq_im * prop_im
        moved_im = freq_im * prop_re - freq_re * prop_im
        return transform(moved_re, moved_im, cosine, -sine)

    row_start = lax.axis_index("lat") * strip
    tops = positions[:, 0] - row_start
    lefts = positions[:, 1]
    extended = padded_2(transmission, (("lat", 2),), half)
    padded = jnp.pad(extended, ((0, 0), (0, 0), (0, 0), (half, half)))

    def cut_window(top, left):
        return lax.dynamic_slice(
            padded, (jnp.int32(0), jnp.int32(0), top, left), (2, slabs, width, width)
        )

    windows = jnp.transpose(jax.vmap(cut_window)(tops, lefts), (2, 0, 1, 3, 4))
    live = (jnp.arange(slots, dtype=jnp.int32) < counts[0]).astype(jnp.float32)
    depth_index = lax.axis_index("depth")
    chain = lax.axis_size("depth")

    def forward_slabs(wave, cuts):

        def forward_step(carry, piece):
            mixed_re = carry[:, 0] * piece[:, 0] - carry[:, 1] * piece[:, 1]
            mixed_im = carry[:, 0] * piece[:, 1] + carry[:, 1] * piece[:, 0]
            new_re, new_im = propagate(mixed_re, mixed_im)
            return (jnp.stack([new_re, new_im], 1), carry)

        return lax.scan(forward_step, wave, cuts)

    def adjoint_slabs(chi, cuts, befores):

        def adjoint_step(carry, inputs):
            piece, before = inputs
            back_re, back_im = back_propagate(carry[:, 0], carry[:, 1])
            term_re = before[:, 0] * back_re + before[:, 1] * back_im
            term_im = before[:, 0] * back_im - before[:, 1] * back_re
            next_re = piece[:, 0] * back_re + piece[:, 1] * back_im
            next_im = piece[:, 0] * back_im - piece[:, 1] * back_re
            return (jnp.stack([next_re, next_im], 1), jnp.stack([term_re, term_im], 1))

        return lax.scan(adjoint_step, chi, (cuts, befores), reverse=True)

    def far_field(exits):
        far_re, far_im = transform(exits[:, 0], exits[:, 1], cosine, sine)
        magnitude = jnp.sqrt(far_re * far_re + far_im * far_im + 1.0)
        weight = live[:, None, None] * (magnitude - amplitude) / magnitude
        back_re, back_im = transform(weight * far_re, weight * far_im, cosine, -sine)
        return jnp.stack([back_re, back_im], 1)

    wave_shape = (slabs, slots, 2, width, width)
    wave = jnp.broadcast_to(probe[None], (slots, 2, width, width))
    stored = jnp.zeros(wave_shape, jnp.float32)
    for section in range(chain):
        if section > 0:
            wave = from_behind(wave, "depth", 1)
        wave, stored = lax.cond(
            depth_index == section,
            lambda w, s: forward_slabs(w, windows),
            lambda w, s: (w, s),
            wave,
            stored,
        )
    chi = lax.cond(depth_index == chain - 1, far_field, jnp.zeros_like, wave)
    terms = jnp.zeros(wave_shape, jnp.float32)
    for section in range(chain):
        if section > 0:
            chi = from_behind(chi, "depth", -1)
        chi, terms = lax.cond(
            depth_index == chain - 1 - section,
            lambda c, g: adjoint_slabs(c, windows, stored),
            lambda c, g: (c, g),
            chi,
            terms,
        )
    buffer = jnp.zeros((2, slabs, strip + width, columns + width), jnp.float32)

    def place(slot, accum):
        piece = jnp.transpose(lax.dynamic_index_in_dim(terms, slot, 1, False), (1, 0, 2, 3))
        start = (jnp.int32(0), jnp.int32(0), tops[slot], lefts[slot])
        current = lax.dynamic_slice(accum, start, (2, slabs, width, width))
        return lax.dynamic_update_slice(accum, current + piece, start)

    buffer = lax.fori_loop(0, slots, place, buffer)
    buffer = buffer[:, :, :, half : half + columns]
    edges = jnp.concatenate([buffer[:, :, :half], buffer[:, :, strip + half :]], axis=2)
    arrived = padded_2(edges, (("lat", 2),), half)
    core = buffer[:, :, half : half + strip]
    core = core.at[:, :, :half].add(arrived[:, :, :half])
    core = core.at[:, :, strip - half :].add(arrived[:, :, 3 * half :])
    return core


def solution(mesh):
    placed = (P(None, "depth", "lat", None), P(), P("lat", None, None), P("lat", None), P("lat"))
    return jax.shard_map(
        on_device,
        mesh=mesh,
        in_specs=placed,
        out_specs=P(None, "depth", "lat", None),
        check_vma=False,
    )
```

profile of v0, /device:TPU:62, one launch (start us, length us, event | category | flops | bytes accessed | tf_op | source)
XLA Modules:
  0.0 229.0 jit_solution(3087926111841438433)
XLA Ops:
  0.0 3.4 %collective-permute-start = (f32[2,2,64,1024]{3,2,1,0:T(8,128)}, f32[2,2,64,1024]{3,2,1,0:T(8,128)S(1)}, u32[]{:S(2)}, u32[]{:S(2)}) collective-permute-start(f32[2,2,64,1024]{3,2,1,0:T(8,128)} %param.33), channel_id=1, source_target_pairs={{0,1},{1,2},{2,3},{3,4},{4,5},{5,6},{6,7},{7,8},{8,9},{9,10},{10,1... | collective-permute-start | bytes 3145736 | tf_op jit(solution)/shard_map/ppermute | solution.py:20
  3.4 2.4 %collective-permute-start.1 = (f32[2,2,64,1024]{3,2,1,0:T(8,128)}, f32[2,2,64,1024]{3,2,1,0:T(8,128)S(1)}, u32[]{:S(2)}, u32[]{:S(2)}) collective-permute-start(f32[2,2,64,1024]{3,2,1,0:T(8,128)} %param.33), channel_id=1, source_target_pairs={{1,0},{2,1},{3,2},{4,3},{5,4},{6,5},{7,6},{8,7},{9,8},{10,9},{11,1... | collective-permute-start | bytes 3145736 | tf_op jit(solution)/shard_map/ppermute | solution.py:22
  5.9 0.8 fusion.179
  7.8 19.2 %collective-permute-done = f32[2,2,64,1024]{3,2,1,0:T(8,128)S(1)} collective-permute-done((f32[2,2,64,1024]{3,2,1,0:T(8,128)}, f32[2,2,64,1024]{3,2,1,0:T(8,128)S(1)}, u32[]{:S(2)}, u32[]{:S(2)}) %collective-permute-start) | collective-permute-done | bytes 1048608 | tf_op jit(solution)/shard_map/ppermute | solution.py:20
  27.0 7.3 %collective-permute-done.1 = f32[2,2,64,1024]{3,2,1,0:T(8,128)S(1)} collective-permute-done((f32[2,2,64,1024]{3,2,1,0:T(8,128)}, f32[2,2,64,1024]{3,2,1,0:T(8,128)S(1)}, u32[]{:S(2)}, u32[]{:S(2)}) %collective-permute-start.1) | collective-permute-done | bytes 1048608 | tf_op jit(solution)/shard_map/ppermute | solution.py:22
  34.3 4.0 %select_maximum_fusion = f32[2,2,192,1152]{3,2,1,0:T(8,128)} fusion(f32[2,2,64,1024]{3,2,1,0:T(8,128)S(1)} %collective-permute-done.1, f32[2,2,64,1024]{3,2,1,0:T(8,128)} %param.33, f32[2,2,64,1024]{3,2,1,0:T(8,128)S(1)} %collective-permute-done), kind=kLoop, calls=%fused_computation.263 | loop fusion | flops 7077888 | bytes 6684672 | tf_op jit(solution)/shard_map/concatenate | solution.py:18
  38.3 12.7 %while.77 = (s32[]{:T(128)}, f32[2,2,192,1152]{3,2,1,0:T(8,128)}, s32[4,4]{1,0:T(4,128)S(1)}, f32[4,2,2,128,128]{4,3,2,1,0:T(8,128)S(1)}, s32[]{:T(128)}) while((s32[]{:T(128)}, f32[2,2,192,1152]{3,2,1,0:T(8,128)}, s32[4,4]{1,0:T(4,128)S(1)}, f32[4,2,2,128,128]{4,3,2,1,0:T(8,128)S(1)}, s32[]{:T(128)}) %tuple.247), condition=%wide.while_cond.2, body=%wide.while_body.2.sunk | while | flops 2 | bytes 524421 | solution.py:96
  38.3 0.6 fusion.382
  39.0 2.5 %bitcast_dynamic-update-slice_fusion.6 = f32[4,2,2,128,128]{4,3,2,1,0:T(8,128)S(1)} fusion(f32[4,2,2,128,128]{4,3,2,1,0:T(8,128)S(1)} %get-tuple-element.2625, s32[]{:T(128)S(6)} %copy.309, f32[2,2,192,1152]{3,2,1,0:T(8,128)} %get-tuple-element.2628, s32[]{:T(128)} %bitcast.639, s32[]{:T(128)} %bitcast.640), kind=kLoop, calls=%fused_computation.259.clone.1 | loop fusion | bytes 524300 | tf_op jit(solution)/shard_map/vmap()/gather
  41.5 0.6 fusion.382
  42.1 2.5 %bitcast_dynamic-update-slice_fusion.6 = f32[4,2,2,128,128]{4,3,2,1,0:T(8,128)S(1)} fusion(f32[4,2,2,128,128]{4,3,2,1,0:T(8,128)S(1)} %get-tuple-element.2625, s32[]{:T(128)S(6)} %copy.309, f32[2,2,192,1152]{3,2,1,0:T(8,128)} %get-tuple-element.2628, s32[]{:T(128)} %bitcast.639, s32[]{:T(128)} %bitcast.640), kind=kLoop, calls=%fused_computation.259.clone.1 | loop fusion | bytes 524300 | tf_op jit(solution)/shard_map/vmap()/gather
  44.7 0.6 fusion.382
  45.3 2.5 %bitcast_dynamic-update-slice_fusion.6 = f32[4,2,2,128,128]{4,3,2,1,0:T(8,128)S(1)} fusion(f32[4,2,2,128,128]{4,3,2,1,0:T(8,128)S(1)} %get-tuple-element.2625, s32[]{:T(128)S(6)} %copy.309, f32[2,2,192,1152]{3,2,1,0:T(8,128)} %get-tuple-element.2628, s32[]{:T(128)} %bitcast.639, s32[]{:T(128)} %bitcast.640), kind=kLoop, calls=%fused_computation.259.clone.1 | loop fusion | bytes 524300 | tf_op jit(solution)/shard_map/vmap()/gather
  47.9 0.6 fusion.382
  48.5 2.5 %bitcast_dynamic-update-slice_fusion.6 = f32[4,2,2,128,128]{4,3,2,1,0:T(8,128)S(1)} fusion(f32[4,2,2,128,128]{4,3,2,1,0:T(8,128)S(1)} %get-tuple-element.2625, s32[]{:T(128)S(6)} %copy.309, f32[2,2,192,1152]{3,2,1,0:T(8,128)} %get-tuple-element.2628, s32[]{:T(128)} %bitcast.639, s32[]{:T(128)} %bitcast.640), kind=kLoop, calls=%fused_computation.259.clone.1 | loop fusion | bytes 524300 | tf_op jit(solution)/shard_map/vmap()/gather
  51.1 21.8 %conditional.5 = (f32[4,2,128,128]{3,2,0,1:T(8,128)S(1)}, f32[2,4,2,128,128]{4,3,1,2,0:T(8,128)}) conditional(s32[]{:T(128)} %convert_element_type.216, f32[4,2,128,128]{3,2,0,1:T(8,128)S(1)} %broadcast_in_dim.65, (f32[128,128]{1,0:T(8,128)S(1)}, f32[128,128]{1,0:T(8,128)S(1)}, f32[128,128]{1,0:T(8,128)S(1)}, f32[128,128]{1,0:T(8,128)S(1)}, ...), branch_computations={%region_0.1_spmd, %region_1.4_spmd} | conditional | flops 1612513280 | bytes 19399116 | solution.py:141
  51.5 21.4 %while.72 = (s32[]{:T(128)}, f32[4,2,128,128]{3,2,0,1:T(8,128)S(1)}, f32[2,4,2,128,128]{4,3,1,2,0:T(8,128)}, f32[2,4,2,128,128]{4,3,0,2,1:T(8,128)S(1)}, f32[128...) while((s32[]{:T(128)}, ...), condition=%wide.region_3.3_spmd, body=%wide.region_2.2_spmd.sunk | while | flops 1612447744 | bytes 18874604 | solution.py:113
  56.4 0.6 fusion.535
  57.0 0.6 fusion.536
  57.6 0.6 fusion.532
  58.2 0.6 fusion.533
  61.3 0.8 bitcast_dynamic-update-slice_fusion.8
  67.1 0.6 fusion.535
  67.7 0.6 fusion.536
  68.9 0.6 fusion.533
  72.0 0.8 bitcast_dynamic-update-slice_fusion.8
  72.8 1.3 collective-permute-start.2
  74.8 0.8 collective-permute-done.2
  76.6 6.2 %conditional.7 = (f32[4,2,128,128]{3,2,0,1:T(8,128)S(1)}) conditional(s32[]{:T(128)} %convert_element_type.217, () %tuple.128, (f32[4]{0:T(128)S(1)}, f32[4,2,128,128]{3,2,0,1:T(8,128)S(1)}, f32[128,128]{1,0:T(8,128)S(1)}, f32[128,128]{1,0:T(8,128)S(1)}, f32[128,128]{1,0:T(8,128)S(1)}, /*index=5*/f32[128,128]{1,0:T(8,128)S(1)}, ...), branch_computations={%region_8.9_spmd, %region_9.10_spmd} | conditional | flops 1612054528 | bytes 15466520 | solution.py:148
  82.8 6.8 %conditional.8 = (f32[4,2,128,128]{3,2,0,1:T(8,128)S(1)}, f32[2,4,2,128,128]{4,3,1,2,0:T(8,128)}) conditional(s32[]{:T(128)} %convert_element_type.217, f32[4,2,128,128]{3,2,0,1:T(8,128)S(1)} %get-tuple-element.2674, (f32[128,128]{1,0:T(8,128)S(1)}, f32[128,128]{1,0:T(8,128)S(1)}, f32[128,128]{1,0:T(8,128)S(1)}, f32[128,128]{1,0:T(8,128)S(1)}, ...), branch_computations={%region_10.11_spmd, %region_11.14_spmd} | conditional | flops 1613037568 | bytes 22021600 | solution.py:153
  82.8 1.1 broadcast.205
  89.6 1.3 collective-permute-start.3
  90.9 42.5 %collective-permute-done.3 = f32[4,2,128,128]{3,2,0,1:T(8,128)S(1)} collective-permute-done((f32[4,2,128,128]{3,2,0,1:T(8,128)S(1)}, f32[4,2,128,128]{3,2,0,1:T(8,128)S(1)}, u32[]{:S(2)}, u32[]{:S(2)}) %collective-permute-start.3) | collective-permute-done | bytes 524320 | tf_op jit(solution)/shard_map/ppermute | solution.py:32
  133.4 23.5 %conditional.9 = (f32[2,4,2,128,128]{4,3,0,2,1:T(8,128)}) conditional(s32[]{:T(128)} %convert_element_type.216, f32[2,4,2,128,128]{4,3,1,2,0:T(8,128)} %get-tuple-element.1137, (f32[128,128]{1,0:T(8,128)S(1)}, f32[128,128]{1,0:T(8,128)S(1)}, f32[128,128]{1,0:T(8,128)S(1)}, f32[128,128]{1,0:T(8,128)S(1)}, f32[2,4,2,128,128]{4,3,0,2,1:T(8,128)S(1)}, ...), branch_computations={%region_14.15_spmd, %region_15.18_spmd} | conditional | flops 1613037568 | bytes 22021592 | solution.py:153
  133.7 1.1 broadcast.207.clone
  134.8 22.2 %while.75 = (s32[]{:T(128)}, f32[4,2,128,128]{3,2,0,1:T(8,128)S(1)}, f32[2,4,2,128,128]{4,3,0,2,1:T(8,128)}, f32[2,4,2,128,128]{4,3,0,2,1:T(8,128)S(1)}, f32[128...) while((s32[]{:T(128)}, ...), condition=%wide.region_17.17_spmd, body=%wide.region_16.16_spmd.sunk | while | flops 1612972032 | bytes 20448500 | solution.py:126
  138.9 0.6 fusion.416
  139.5 0.6 fusion.417
  140.2 0.6 fusion.413
  140.8 0.6 fusion.414
  143.2 1.1 copy_bitcast_fusion.8
  144.3 0.6 add_bitcast_fusion.6
  145.0 0.9 copy_dynamic-update-slice_fusion.2
  150.6 0.6 fusion.417
  151.8 0.6 fusion.414
  154.2 1.1 copy_bitcast_fusion.8
  155.4 0.6 add_bitcast_fusion.6
  156.1 0.9 copy_dynamic-update-slice_fusion.2
  156.9 2.0 broadcast_in_dim.64
  158.9 42.1 %while.76 = (s32[]{:T(128)}, f32[2,2,192,1152]{3,2,1,0:T(8,128)}, s32[4]{0:T(128)S(1)}, s32[4]{0:T(128)S(1)}, f32[2,4,2,128,128]{4,3,0,2,1:T(8,128)}, /*index=5*/s32[]{:T(128)}, s32[]{:T(128)}, s32[]{:T(128)}, s32[]{:T(128)}) while((s32[]{:T(128)}, f32[2,2,192,1152]{3,2,1,0:T(8,128)}, s32[4]{0:T(128)S(1)}, s32[4]{0:T(128)S(1)}, ...), condition=%wide.region_19.20_spmd, body=%wide.region_18.19_spmd.sunk | while | flops 65544 | bytes 1310929 | solution.py:168
  164.0 1.3 bitcast_add_fusion.2
  165.3 4.3 %dynamic_update_slice.43 = f32[2,2,192,1152]{3,2,1,0:T(8,128)} dynamic-update-slice(f32[2,2,192,1152]{3,2,1,0:T(8,128)} %get-tuple-element.2656, f32[2,2,128,128]{3,2,1,0:T(8,128)S(1)} %bitcast_add_fusion.2, s32[]{:T(128)} %constant.266.clone.1..sunk, s32[]{:T(128)} %constant.266.clone.1..sunk, s32[]{:T(128)S(6)} %select_n.267, s32[]{:T(128)S(6)} %select_n.268) | dynamic-update-slice | bytes 524292 | tf_op jit(solution)/shard_map/while/body/eval_jaxpr/dynamic_update_slice | solution.py:166
  174.6 1.3 bitcast_add_fusion.2
  175.9 4.2 %dynamic_update_slice.43 = f32[2,2,192,1152]{3,2,1,0:T(8,128)} dynamic-update-slice(f32[2,2,192,1152]{3,2,1,0:T(8,128)} %get-tuple-element.2656, f32[2,2,128,128]{3,2,1,0:T(8,128)S(1)} %bitcast_add_fusion.2, s32[]{:T(128)} %constant.266.clone.1..sunk, s32[]{:T(128)} %constant.266.clone.1..sunk, s32[]{:T(128)S(6)} %select_n.267, s32[]{:T(128)S(6)} %select_n.268) | dynamic-update-slice | bytes 524292 | tf_op jit(solution)/shard_map/while/body/eval_jaxpr/dynamic_update_slice | solution.py:166
  185.2 1.3 bitcast_add_fusion.2
  186.5 4.1 %dynamic_update_slice.43 = f32[2,2,192,1152]{3,2,1,0:T(8,128)} dynamic-update-slice(f32[2,2,192,1152]{3,2,1,0:T(8,128)} %get-tuple-element.2656, f32[2,2,128,128]{3,2,1,0:T(8,128)S(1)} %bitcast_add_fusion.2, s32[]{:T(128)} %constant.266.clone.1..sunk, s32[]{:T(128)} %constant.266.clone.1..sunk, s32[]{:T(128)S(6)} %select_n.267, s32[]{:T(128)S(6)} %select_n.268) | dynamic-update-slice | bytes 524292 | tf_op jit(solution)/shard_map/while/body/eval_jaxpr/dynamic_update_slice | solution.py:166
  195.6 1.3 bitcast_add_fusion.2
  196.9 4.1 %dynamic_update_slice.43 = f32[2,2,192,1152]{3,2,1,0:T(8,128)} dynamic-update-slice(f32[2,2,192,1152]{3,2,1,0:T(8,128)} %get-tuple-element.2656, f32[2,2,128,128]{3,2,1,0:T(8,128)S(1)} %bitcast_add_fusion.2, s32[]{:T(128)} %constant.266.clone.1..sunk, s32[]{:T(128)} %constant.266.clone.1..sunk, s32[]{:T(128)S(6)} %select_n.267, s32[]{:T(128)S(6)} %select_n.268) | dynamic-update-slice | bytes 524292 | tf_op jit(solution)/shard_map/while/body/eval_jaxpr/dynamic_update_slice | solution.py:166
  201.1 2.2 fusion.178
  203.3 1.9 collective-permute-start.4
  205.2 3.9 %collective-permute-start.5 = (f32[2,2,64,1024]{3,2,1,0:T(8,128)S(1)}, f32[2,2,64,1024]{3,2,1,0:T(8,128)S(1)}, u32[]{:S(2)}, u32[]{:S(2)}) collective-permute-start(f32[2,2,64,1024]{3,2,1,0:T(8,128)S(1)} %get-tuple-element.1618), channel_id=1, source_target_pairs={{1,0},{2,1},{3,2},{4,3},{5,4},{6,5},{7,6},{8,7},{9,8},{10,9},{11,1... | collective-permute-start | bytes 3145736 | tf_op jit(solution)/shard_map/ppermute | solution.py:22
  209.1 10.8 %collective-permute-done.4 = f32[2,2,64,1024]{3,2,1,0:T(8,128)S(1)} collective-permute-done((f32[2,2,64,1024]{3,2,1,0:T(8,128)S(1)}, f32[2,2,64,1024]{3,2,1,0:T(8,128)S(1)}, u32[]{:S(2)}, u32[]{:S(2)}) %collective-permute-start.4) | collective-permute-done | bytes 1048608 | tf_op jit(solution)/shard_map/ppermute | solution.py:20
  220.0 6.1 %collective-permute-done.5 = f32[2,2,64,1024]{3,2,1,0:T(8,128)S(1)} collective-permute-done((f32[2,2,64,1024]{3,2,1,0:T(8,128)S(1)}, f32[2,2,64,1024]{3,2,1,0:T(8,128)S(1)}, u32[]{:S(2)}, u32[]{:S(2)}) %collective-permute-start.5) | collective-permute-done | bytes 1048608 | tf_op jit(solution)/shard_map/ppermute | solution.py:22
  226.1 2.6 %add_add_fusion = f32[2,2,64,1024]{3,2,1,0:T(8,128)} fusion(f32[2,2,64,1024]{3,2,1,0:T(8,128)S(1)} %collective-permute-done.5, f32[2,2,64,1024]{3,2,1,0:T(8,128)S(1)} %collective-permute-done.4, f32[2,2,192,1152]{3,2,1,0:T(8,128)} %get-tuple-element.1139), kind=kLoop, calls=%fused_computation.266 | loop fusion | flops 524288 | bytes 4194304 | tf_op jit(solution)/shard_map/add | solution.py:174
  (101 shorter events, 35.1 us)
Async XLA Ops:
  0.0 27.0 %collective-permute-start = (f32[2,2,64,1024]{3,2,1,0:T(8,128)}, f32[2,2,64,1024]{3,2,1,0:T(8,128)S(1)}, u32[]{:S(2)}, u32[]{:S(2)}) collective-permute-start(f32[2,2,64,1024]{3,2,1,0:T(8,128)} %param.33), channel_id=1, source_target_pairs={{0,1},{1,2},{2,3},{3,4},{4,5},{5,6},{6,7},{7,8},{8,9},{9,10},{10,1... | collective-permute-start | bytes 3145736 | tf_op jit(solution)/shard_map/ppermute | solution.py:20
  3.4 30.9 %collective-permute-start.1 = (f32[2,2,64,1024]{3,2,1,0:T(8,128)}, f32[2,2,64,1024]{3,2,1,0:T(8,128)S(1)}, u32[]{:S(2)}, u32[]{:S(2)}) collective-permute-start(f32[2,2,64,1024]{3,2,1,0:T(8,128)} %param.33), channel_id=1, source_target_pairs={{1,0},{2,1},{3,2},{4,3},{5,4},{6,5},{7,6},{8,7},{9,8},{10,9},{11,1... | collective-permute-start | bytes 3145736 | tf_op jit(solution)/shard_map/ppermute | solution.py:22
  7.8 43.2 %copy-start.1 = (f32[2,128,128]{2,1,0:T(8,128)S(1)}, f32[2,128,128]{2,1,0:T(8,128)}, u32[]{:S(2)}) copy-start(f32[2,128,128]{2,1,0:T(8,128)} %param.34) | copy-start | bytes 393220
  72.8 2.8 %collective-permute-start.2 = (f32[4,2,128,128]{3,2,0,1:T(8,128)S(1)}, f32[4,2,128,128]{3,2,0,1:T(8,128)S(1)}, u32[]{:S(2)}, u32[]{:S(2)}) collective-permute-start(f32[4,2,128,128]{3,2,0,1:T(8,128)S(1)} %get-tuple-element.1133), channel_id=1, source_target_pairs={{0,64},{1,65},{2,66},{3,67},{4,68},{5,69},{6,70},{7,71},{8,72},{9,... | collective-permute-start | bytes 1572872 | tf_op jit(solution)/shard_map/ppermute | solution.py:32
  75.7 0.9 copy-start
  89.6 43.8 %collective-permute-start.3 = (f32[4,2,128,128]{3,2,0,1:T(8,128)S(1)}, f32[4,2,128,128]{3,2,0,1:T(8,128)S(1)}, u32[]{:S(2)}, u32[]{:S(2)}) collective-permute-start(f32[4,2,128,128]{3,2,0,1:T(8,128)S(1)} %get-tuple-element.1138), channel_id=1, source_target_pairs={{64,0},{65,1},{66,2},{67,3},{68,4},{69,5},{70,6},{71,7},{72,8},{73... | collective-permute-start | bytes 1572872 | tf_op jit(solution)/shard_map/ppermute | solution.py:32
  203.3 16.7 %collective-permute-start.4 = (f32[2,2,64,1024]{3,2,1,0:T(8,128)S(1)}, f32[2,2,64,1024]{3,2,1,0:T(8,128)S(1)}, u32[]{:S(2)}, u32[]{:S(2)}) collective-permute-start(f32[2,2,64,1024]{3,2,1,0:T(8,128)S(1)} %get-tuple-element.1617), channel_id=1, source_target_pairs={{0,1},{1,2},{2,3},{3,4},{4,5},{5,6},{6,7},{7,8},{8,9},{9,10},{10,1... | collective-permute-start | bytes 3145736 | tf_op jit(solution)/shard_map/ppermute | solution.py:20
  205.2 20.9 %collective-permute-start.5 = (f32[2,2,64,1024]{3,2,1,0:T(8,128)S(1)}, f32[2,2,64,1024]{3,2,1,0:T(8,128)S(1)}, u32[]{:S(2)}, u32[]{:S(2)}) collective-permute-start(f32[2,2,64,1024]{3,2,1,0:T(8,128)S(1)} %get-tuple-element.1618), channel_id=1, source_target_pairs={{1,0},{2,1},{3,2},{4,3},{5,4},{6,5},{7,6},{8,7},{9,8},{10,9},{11,1... | collective-permute-start | bytes 3145736 | tf_op jit(solution)/shard_map/ppermute | solution.py:22
where the time goes:
time: 233 us; the launch traced here: 229 us
  waiting for transfers between devices  86.8 us (37%)
  local copies, waits for them, and re-layouts  46.4 us (20%)
  matrix products  36.4 us (16%)
  loops' own time  29.3 us (13%)
  other arithmetic  14.8 us (6%)
  starting transfers between devices  14.3 us (6%)
    ppermute x2, waiting for transfers between devices, from_behind(): lax.ppermute(value, axis, [(source, source + steps) for source in range(l...  43.3 us
    ppermute x2, waiting for transfers between devices, padded_2(): lax.ppermute(tail, axis, [(i, (i + 1) % count) for i in range(ends)])  30 us
    dot_general x32, matrix products, right_mul(): return jnp.einsum('pjk,kl->pjl', values, table, precision=HIGHEST)  18.9 us
    dot_general x32, matrix products, left_mul(): return jnp.einsum('jk,pkl->pjl', table, values, precision=HIGHEST)  17.4 us
    dynamic_update_slice x4, local copies, waits for them, and re-layouts, place(): return lax.dynamic_update_slice(accum, current + piece, start)  16.7 us
    another operation x1, loops' own time, on_device(): buffer = lax.fori_loop(0, slots, place, buffer)  15.6 us
    ppermute x2, waiting for transfers between devices, padded_2(): lax.ppermute(head, axis, [((i + 1) % count, i) for i in range(ends)])  13.5 us
    gather x12, local copies, waits for them, and re-layouts  12.6 us
  transfers between devices with their start and end apart: 6, of which 6 were waited for; matrix products, arithmetic and copies ran while one was open for 1% of the time, Pallas kernels for 0%

commit v1 on v0

v1 whole, which is shorter than its diff:
```python
import functools

import jax
import jax.numpy as jnp
import ml_dtypes
import numpy as np
from jax import lax
from jax.experimental import pallas as pl
from jax.experimental.pallas import tpu as pltpu
from jax.sharding import PartitionSpec as P

PROP_COEF = 40.0
WIN = 128
HALF = 64
MESH = pl.DeviceIdType.MESH
PROP, PROP_CONJ, DFT, DFT_CONJ = range(4)


def tables():
    index = np.arange(WIN)
    dft = np.exp(-2j * np.pi * (np.outer(index, index) % WIN) / WIN) / np.sqrt(WIN)
    freq = ((index + WIN // 2) % WIN - WIN // 2) / WIN
    prop = dft.conj() @ np.diag(np.exp(-1j * PROP_COEF * freq * freq)) @ dft
    terms = []
    for matrix in (prop, prop.conj(), dft, dft.conj()):
        real = np.block([[matrix.real, -matrix.imag], [matrix.imag, matrix.real]])
        high = real.astype(ml_dtypes.bfloat16)
        low = (real - high.astype(np.float64)).astype(ml_dtypes.bfloat16)
        terms.append(np.stack([high, low]))
    return np.stack(terms)


def split(values):
    high = values.astype(jnp.bfloat16)
    low = (values - high.astype(jnp.float32)).astype(jnp.bfloat16)
    return high, low


def product(mats, which, re, im):
    conj = which ^ 1
    high, low = split(jnp.concatenate([re, im], axis=1))
    right = jnp.concatenate([mats[conj, 0], mats[conj, 0], mats[conj, 1]], axis=0)
    first = jnp.dot(
        jnp.concatenate([high, low, high], axis=1), right, preferred_element_type=jnp.float32
    )
    high, low = split(jnp.concatenate([first[:, :WIN], first[:, WIN:]], axis=0))
    left = jnp.concatenate([mats[which, 0], mats[which, 0], mats[which, 1]], axis=1)
    second = jnp.dot(
        left, jnp.concatenate([high, low, high], axis=0), preferred_element_type=jnp.float32
    )
    return second[:WIN], second[WIN:]


def column_block(pos, slot):
    column = pos[slot, 1] + HALF
    return lax.shift_right_logical(column, 7), column & (WIN - 1)


def cut(tile, pos, slot):
    block, lane = column_block(pos, slot)
    lanes = lax.broadcasted_iota(jnp.int32, (2, 2, HALF, WIN), 3)
    return jnp.where(lanes >= lane, tile[block], tile[block + 1])


def kernel(
    n, pos, counts, trans, probe, amp, mats_hbm,
    from_prev, from_next, own, pos_prev_out, pos_next_out,
    tile, mats, to_prev, to_next, have_prev, have_next, window, waves,
    wave_out, wave_in, top, bottom, pos_prev, pos_next,
    tile_sem, mats_sem, pos_send, pos_recv, win_send, win_recv, wave_send, wave_recv,
    grad_send, grad_recv, own_sem,
):
    core = lax.axis_index("depth")
    lat = lax.axis_index("lat")
    has_prev = lat > 0
    has_next = lat < n - 1
    slots = pos.shape[0]
    blocks = tile.shape[0] - 2
    partner = (1 - core, lat)
    sides = ((0, has_prev, (core, lat - 1)), (1, has_next, (core, lat + 1)))

    loads = [
        pltpu.make_async_copy(
            trans.at[:, :, :, pl.ds(k * WIN, WIN)], tile.at[k + 1], tile_sem.at[k]
        )
        for k in range(blocks)
    ]
    for load in loads:
        load.start()
    mats_load = pltpu.make_async_copy(mats_hbm, mats, mats_sem)
    mats_load.start()

    barrier = pltpu.get_barrier_semaphore()
    pl.semaphore_signal(barrier, inc=1, device_id=partner, device_id_type=MESH)
    for _, there, device in sides:
        @pl.when(there)
        def _():
            pl.semaphore_signal(barrier, inc=1, device_id=device, device_id_type=MESH)

    tile[0] = jnp.zeros(tile.shape[1:], jnp.float32)
    tile[blocks + 1] = jnp.zeros(tile.shape[1:], jnp.float32)

    @pl.when(jnp.logical_not(has_prev))
    def _():
        have_prev[...] = jnp.zeros_like(have_prev)
        for k in range(4):
            pos_prev[k, 0] = 0
            pos_prev[k, 1] = 0

    @pl.when(jnp.logical_not(has_next))
    def _():
        have_next[...] = jnp.zeros_like(have_next)
        for k in range(4):
            pos_next[k, 0] = 0
            pos_next[k, 1] = 0

    pl.semaphore_wait(barrier, 1 + has_prev.astype(jnp.int32) + has_next.astype(jnp.int32))

    def pos_copy(side, device):
        landing = (pos_next, pos_prev)[side]
        return pltpu.make_async_remote_copy(
            src_ref=pos, dst_ref=landing, send_sem=pos_send.at[side], recv_sem=pos_recv.at[1 - side],
            device_id=device, device_id_type=MESH,
        )

    def pos_arrival(side, device):
        landing = (pos_prev, pos_next)[side]
        return pltpu.make_async_remote_copy(
            src_ref=pos, dst_ref=landing, send_sem=pos_send.at[side], recv_sem=pos_recv.at[side],
            device_id=device, device_id_type=MESH,
        )

    def win_copy(side, slot, device):
        source = (to_prev, to_next)[side]
        landing = (have_next, have_prev)[side]
        return pltpu.make_async_remote_copy(
            src_ref=source.at[slot], dst_ref=landing.at[slot],
            send_sem=win_send.at[side, slot], recv_sem=win_recv.at[1 - side, slot],
            device_id=device, device_id_type=MESH,
        )

    def win_arrival(side, slot, device):
        landing = (have_prev, have_next)[side]
        return pltpu.make_async_remote_copy(
            src_ref=to_prev.at[slot], dst_ref=landing.at[slot],
            send_sem=win_send.at[side, slot], recv_sem=win_recv.at[side, slot],
            device_id=device, device_id_type=MESH,
        )

    def grad_copy(side, slot, device):
        landing = (from_next, from_prev)[side]
        return pltpu.make_async_remote_copy(
            src_ref=top.at[slot], dst_ref=landing.at[slot],
            send_sem=grad_send.at[side, slot], recv_sem=grad_recv.at[1 - side, slot],
            device_id=device, device_id_type=MESH,
        )

    def grad_arrival(side, slot, device):
        landing = (from_prev, from_next)[side]
        return pltpu.make_async_remote_copy(
            src_ref=top.at[slot], dst_ref=landing.at[slot],
            send_sem=grad_send.at[side, slot], recv_sem=grad_recv.at[side, slot],
            device_id=device, device_id_type=MESH,
        )

    def wave_copy(slot):
        return pltpu.make_async_remote_copy(
            src_ref=wave_out.at[slot], dst_ref=wave_in.at[slot],
            send_sem=wave_send.at[slot], recv_sem=wave_recv.at[slot],
            device_id=partner, device_id_type=MESH,
        )

    def own_copy(slot):
        return pltpu.make_async_copy(bottom.at[slot], own.at[slot], own_sem.at[slot])

    for side, there, device in sides:
        @pl.when(there)
        def _():
            pos_copy(side, device).start()

    for load in loads:
        load.wait()
    for side, there, device in sides:
        @pl.when(there)
        def _():
            pos_arrival(side, device).wait_recv()

    def send_windows(slot, carry):
        for side, there, device in sides:
            buffer = (to_prev, to_next)[side]
            theirs = (pos_prev, pos_next)[side]

            @pl.when(there)
            def _():
                buffer[slot] = cut(tile, theirs, slot)
                win_copy(side, slot, device).start()

        return carry

    lax.fori_loop(0, slots, send_windows, 0)

    def build_window(slot):
        for side, there, device in sides:
            @pl.when(there)
            def _():
                win_arrival(side, slot, device).wait_recv()

        row = pos[slot, 0] - lat * HALF
        rows = lax.broadcasted_iota(jnp.int32, (2, 2, HALF, WIN), 2)
        window[slot, :, :, :HALF] = jnp.where(rows >= row, have_prev[slot], have_next[slot])
        window[slot, :, :, HALF:] = cut(tile, pos, slot)

    def times(slot, layer, re, im):
        t_re, t_im = window[slot, 0, layer], window[slot, 1, layer]
        return re * t_re - im * t_im, re * t_im + im * t_re

    def times_conj(slot, layer, re, im):
        t_re, t_im = window[slot, 0, layer], window[slot, 1, layer]
        return re * t_re + im * t_im, im * t_re - re * t_im

    def store_term(slot, layer, re, im):
        p_re, p_im = waves[slot, layer, 0], waves[slot, layer, 1]
        term_re = p_re * re + p_im * im
        term_im = p_re * im - p_im * re
        top[slot, 0, layer] = term_re[:HALF]
        top[slot, 1, layer] = term_im[:HALF]
        bottom[slot, 0, layer] = term_re[HALF:]
        bottom[slot, 1, layer] = term_im[HALF:]

    def send_terms(slot):
        for side, there, device in sides:
            @pl.when(there)
            def _():
                grad_copy(side, slot, device).start()

        own_copy(slot).start()

    mats_load.wait()

    @pl.when(core == 0)
    def _():
        def forward(slot):
            build_window(slot)
            row = pos[slot, 0] - lat * HALF
            _, lane = column_block(pos, slot)
            re = pltpu.roll(pltpu.roll(probe[0], row, 0), lane, 1)
            im = pltpu.roll(pltpu.roll(probe[1], row, 0), lane, 1)
            waves[slot, 0, 0] = re
            waves[slot, 0, 1] = im
            re, im = product(mats, PROP, *times(slot, 0, re, im))
            waves[slot, 1, 0] = re
            waves[slot, 1, 1] = im
            re, im = product(mats, PROP, *times(slot, 1, re, im))
            wave_out[slot, 0] = re
            wave_out[slot, 1] = im
            wave_copy(slot).start()

        def backward(slot):
            wave_copy(slot).wait_recv()
            re, im = product(mats, PROP_CONJ, wave_in[slot, 0], wave_in[slot, 1])
            store_term(slot, 1, re, im)
            re, im = product(mats, PROP_CONJ, *times_conj(slot, 1, re, im))
            store_term(slot, 0, re, im)
            send_terms(slot)

        def step(at, carry):
            @pl.when(at < slots)
            def _():
                forward(at)

            @pl.when(at >= 2)
            def _():
                backward(at - 2)

            return carry

        lax.fori_loop(0, slots + 2, step, 0)

    @pl.when(core == 1)
    def _():
        def whole(slot, carry):
            build_window(slot)
            wave_copy(slot).wait_recv()
            re, im = wave_in[slot, 0], wave_in[slot, 1]
            waves[slot, 0, 0] = re
            waves[slot, 0, 1] = im
            re, im = product(mats, PROP, *times(slot, 0, re, im))
            waves[slot, 1, 0] = re
            waves[slot, 1, 1] = im
            re, im = product(mats, DFT, *times(slot, 1, re, im))
            live = jnp.where(slot < counts[0], 1.0, 0.0).astype(jnp.float32)
            weight = live * (1.0 - amp[slot] / jnp.sqrt(re * re + im * im + 1.0))
            re, im = product(mats, DFT_CONJ, weight * re, weight * im)
            store_term(slot, 1, re, im)
            re, im = product(mats, PROP_CONJ, *times_conj(slot, 1, re, im))
            store_term(slot, 0, re, im)
            re, im = times_conj(slot, 0, re, im)
            wave_out[slot, 0] = re
            wave_out[slot, 1] = im
            wave_copy(slot).start()
            send_terms(slot)
            return carry

        lax.fori_loop(0, slots, whole, 0)

    for k in range(4):
        pos_prev_out[k, 0] = pos_prev[k, 0]
        pos_prev_out[k, 1] = pos_prev[k, 1]
        pos_next_out[k, 0] = pos_next[k, 0]
        pos_next_out[k, 1] = pos_next[k, 1]

    def finish(slot, carry):
        own_copy(slot).wait()
        wave_copy(slot).wait_send()
        for side, there, device in sides:
            @pl.when(there)
            def _():
                win_copy(side, slot, device).wait_send()
                grad_copy(side, slot, device).wait_send()
                grad_arrival(side, slot, device).wait_recv()

        return carry

    for side, there, device in sides:
        @pl.when(there)
        def _():
            pos_copy(side, device).wait_send()

    lax.fori_loop(0, slots, finish, 0)


def place_kernel(n, pos, pos_prev, pos_next, own, from_prev, from_next, out, sums):
    lat = lax.axis_index("lat")
    blocks = sums.shape[0] - 2
    sums[...] = jnp.zeros_like(sums)
    shape = (2, 2, HALF, WIN)
    rows = lax.broadcasted_iota(jnp.int32, shape, 2)
    lanes = lax.broadcasted_iota(jnp.int32, shape, 3)

    def add(where, slot, piece, keep):
        block, lane = column_block(where, slot)
        if keep is not None:
            piece = jnp.where(keep, piece, 0.0)
        sums[block] += jnp.where(lanes >= lane, piece, 0.0)
        sums[block + 1] += jnp.where(lanes >= lane, 0.0, piece)

    def one(slot, carry):
        add(pos, slot, own[slot], None)

        @pl.when(lat > 0)
        def _():
            row = pos_prev[slot, 0] - (lat - 1) * HALF
            add(pos_prev, slot, from_prev[slot], rows < row)

        @pl.when(lat < n - 1)
        def _():
            row = pos_next[slot, 0] - (lat + 1) * HALF
            add(pos_next, slot, from_next[slot], rows >= row)

        return carry

    lax.fori_loop(0, pos.shape[0], one, 0)
    for k in range(blocks):
        out[:, :, :, k * WIN : (k + 1) * WIN] = sums[k + 1]


def on_device(n, trans, probe, amp, pos, counts):
    slots = pos.shape[0]
    blocks = trans.shape[3] // WIN
    smem = pl.BlockSpec(memory_space=pltpu.SMEM)
    vmem = pl.BlockSpec(memory_space=pltpu.VMEM)
    any_space = pl.BlockSpec(memory_space=pl.ANY)
    piece = (slots, 2, 2, HALF, WIN)
    wave = (slots, 2, WIN, WIN)
    f32 = jnp.float32
    mats = jnp.asarray(tables())
    from_prev, from_next, own, pos_prev, pos_next = pl.pallas_call(
        functools.partial(kernel, n),
        out_shape=[jax.ShapeDtypeStruct(piece, f32)] * 3 + [jax.ShapeDtypeStruct(pos.shape, jnp.int32)] * 2,
        in_specs=[smem, smem, any_space, vmem, vmem, any_space],
        out_specs=[any_space, any_space, any_space, smem, smem],
        scratch_shapes=[
            pltpu.VMEM((blocks + 2, 2, 2, HALF, WIN), f32),
            pltpu.VMEM(mats.shape, jnp.bfloat16),
            pltpu.VMEM(piece, f32),
            pltpu.VMEM(piece, f32),
            pltpu.VMEM(piece, f32),
            pltpu.VMEM(piece, f32),
            pltpu.VMEM((slots, 2, 2, WIN, WIN), f32),
            pltpu.VMEM((slots, 2, 2, WIN, WIN), f32),
            pltpu.VMEM(wave, f32),
            pltpu.VMEM(wave, f32),
            pltpu.VMEM(piece, f32),
            pltpu.VMEM(piece, f32),
            pltpu.SMEM(pos.shape, jnp.int32),
            pltpu.SMEM(pos.shape, jnp.int32),
            pltpu.SemaphoreType.DMA((blocks,)),
            pltpu.SemaphoreType.DMA(()),
            pltpu.SemaphoreType.DMA((2,)),
            pltpu.SemaphoreType.DMA((2,)),
            pltpu.SemaphoreType.DMA((2, slots)),
            pltpu.SemaphoreType.DMA((2, slots)),
            pltpu.SemaphoreType.DMA((slots,)),
            pltpu.SemaphoreType.DMA((slots,)),
            pltpu.SemaphoreType.DMA((2, slots)),
            pltpu.SemaphoreType.DMA((2, slots)),
            pltpu.SemaphoreType.DMA((slots,)),
        ],
        compiler_params=pltpu.CompilerParams(
            collective_id=0, has_side_effects=True, vmem_limit_bytes=40 << 20
        ),
        name="windows",
    )(pos, counts, trans, probe, amp, mats)
    return pl.pallas_call(
        functools.partial(place_kernel, n),
        out_shape=jax.ShapeDtypeStruct(trans.shape, f32),
        in_specs=[smem, smem, smem, vmem, vmem, vmem],
        out_specs=vmem,
        scratch_shapes=[pltpu.VMEM((blocks + 2, 2, 2, HALF, WIN), f32)],
        compiler_params=pltpu.CompilerParams(vmem_limit_bytes=40 << 20),
        name="place",
    )(pos, pos_prev, pos_next, own, from_prev, from_next)


def solution(mesh):
    placed = (P(None, "depth", "lat", None), P(), P("lat", None, None), P("lat", None), P("lat"))
    return jax.shard_map(
        functools.partial(on_device, mesh.shape["lat"]),
        mesh=mesh,
        in_specs=placed,
        out_specs=P(None, "depth", "lat", None),
        check_vma=False,
    )
```

time: 233 us -> 45.9 us (0.20)
  the two profiles are of different devices: /device:TPU:62 before, /device:TPU:96 now
where the time goes in v1:
time: 45.9 us; the launch traced here: 45.6 us
  Pallas kernels  40.5 us (88%)
  local copies, waits for them, and re-layouts  4.41 us (10%)
  between operations  0.68 us (1%)
    pallas_call x1, Pallas kernels, on_device(): pl.pallas_call(functools.partial(kernel, n), out_shape=[jax.ShapeDtypeStr...  38.4 us
    unnamed x11, local copies, waits for them, and re-layouts  4.41 us
    pallas_call x1, Pallas kernels, on_device(): pl.pallas_call(functools.partial(place_kernel, n), out_shape=jax.ShapeDty...  2.16 us

profile of v1, /device:TPU:96, one launch (start us, length us, event | category | flops | bytes accessed | tf_op | source)
XLA Modules:
  0.0 45.6 jit_solution(1575912970267429987)
XLA Ops:
  0.0 0.0 copy-start.4
  0.7 0.0 copy-done.4
  0.7 0.1 copy.8.pos
  0.8 0.0 copy-start
  0.8 1.2 %copy-done = f32[2,2,64,1024]{3,2,1,0:T(8,128)S(1)} copy-done((f32[2,2,64,1024]{3,2,1,0:T(8,128)S(1)}, f32[2,2,64,1024]{3,2,1,0:T(8,128)}, u32[]{:S(2)}) %copy-start) | copy-done | bytes 1048600
  2.0 0.0 copy-start.1
  2.0 1.2 %copy-done.1 = bf16[4,2,256,256]{3,2,1,0:T(8,128)(2,1)S(1)} copy-done((bf16[4,2,256,256]{3,2,1,0:T(8,128)(2,1)S(1)}, bf16[4,2,256,256]{3,2,1,0:T(8,128)(2,1)}, u32[]{:S(2)}) %copy-start.1) | copy-done | bytes 1048600
  3.2 0.0 copy-start.2
  3.2 0.9 %copy-done.2 = f32[4,128,128]{2,1,0:T(8,128)S(1)} copy-done((f32[4,128,128]{2,1,0:T(8,128)S(1)}, f32[4,128,128]{2,1,0:T(8,128)}, u32[]{:S(2)}) %copy-start.2) | copy-done | bytes 262168
  4.2 0.0 copy-start.3
  4.2 0.9 %copy-done.3 = f32[2,128,128]{2,1,0:T(8,128)S(1)} copy-done((f32[2,128,128]{2,1,0:T(8,128)S(1)}, f32[2,128,128]{2,1,0:T(8,128)}, u32[]{:S(2)}) %copy-start.3) | copy-done | bytes 131096
  5.1 38.4 %windows.1 = (f32[4,2,2,64,128]{4,3,2,1,0:T(8,128)S(1)}, f32[4,2,2,64,128]{4,3,2,1,0:T(8,128)S(1)}, f32[4,2,2,64,128]{4,3,2,1,0:T(8,128)S(1)}, s32[4,2]{1,0:T(4,128)S(1)}, s32[4,2]{1,0:T(4,128)S(1)}) custom-call(s32[4,2]{1,0:T(4,128)S(1)} %copy.8.pos, s32[1]{0:T(128)S(6)} %copy.9.counts, f32[2,2,64,1024]{3,2,1,0:T(8,128)S(1)} %copy-done, ...), custom_call_target="tpu_custom_call" | custom-call | tf_op jit(solution)/shard_map/windows/pallas_call | solution.py:377
  43.5 2.2 %place.1 = f32[2,2,64,1024]{3,2,1,0:T(8,128)} custom-call(s32[4,2]{1,0:T(4,128)S(1)} %copy.8.pos, s32[4,2]{1,0:T(4,128)S(1)} %get-tuple-element.10.pos_prev, s32[4,2]{1,0:T(4,128)S(1)} %get-tuple-element.11.pos_next, f32[4,2,2,64,128]{4,3,2,1,0:T(8,128)S(1)} %get-tuple-element.12.own, f32[4,2,2,64,128]{4,3,2,1,0:T(8,128)S(1)} %get-tuple-element.13.from_prev, ...), custom_call_target="tpu_custom_call" | custom-call | tf_op jit(solution)/shard_map/place/pallas_call | solution.py:414
Async XLA Ops:
  0.0 0.7 %copy-start.4 = (s32[4,2]{0,1:T(2,128)S(1)}, s32[4,2]{0,1:T(2,128)}, u32[]{:S(2)}) copy-start(s32[4,2]{0,1:T(2,128)} %param.9) | copy-start | bytes 100
  0.8 1.2 %copy-start = (f32[2,2,64,1024]{3,2,1,0:T(8,128)S(1)}, f32[2,2,64,1024]{3,2,1,0:T(8,128)}, u32[]{:S(2)}) copy-start(f32[2,2,64,1024]{3,2,1,0:T(8,128)} %trans.1) | copy-start | bytes 3145732
  2.0 1.2 %copy-start.1 = (bf16[4,2,256,256]{3,2,1,0:T(8,128)(2,1)S(1)}, bf16[4,2,256,256]{3,2,1,0:T(8,128)(2,1)}, u32[]{:S(2)}) copy-start(bf16[4,2,256,256]{3,2,1,0:T(8,128)(2,1)} %constant.2.clone.mats_hbm) | copy-start | bytes 3145732
  3.2 0.9 %copy-start.2 = (f32[4,128,128]{2,1,0:T(8,128)S(1)}, f32[4,128,128]{2,1,0:T(8,128)}, u32[]{:S(2)}) copy-start(f32[4,128,128]{2,1,0:T(8,128)} %amp.1) | copy-start | bytes 786436
  4.2 0.9 %copy-start.3 = (f32[2,128,128]{2,1,0:T(8,128)S(1)}, f32[2,128,128]{2,1,0:T(8,128)}, u32[]{:S(2)}) copy-start(f32[2,128,128]{2,1,0:T(8,128)} %probe.1) | copy-start | bytes 393220

commit v2 on v1

--- a/solution.py
+++ b/solution.py
@@ -52,7 +52,7 @@
 
 
 def column_block(pos, slot):
-    column = pos[slot, 1] + HALF
+    column = pos[1, slot] + HALF
     return lax.shift_right_logical(column, 7), column & (WIN - 1)
 
 
@@ -63,22 +63,28 @@
 
 
 def kernel(
-    n, pos, counts, trans, probe, amp, mats_hbm,
-    from_prev, from_next, own, pos_prev_out, pos_next_out,
-    tile, mats, to_prev, to_next, have_prev, have_next, window, waves,
-    wave_out, wave_in, top, bottom, pos_prev, pos_next,
-    tile_sem, mats_sem, pos_send, pos_recv, win_send, win_recv, wave_send, wave_recv,
+    n, pos_hbm, counts_hbm, trans, probe_hbm, amp_hbm, mats_hbm,
+    from_prev, from_next, own, pos_out,
+    tile, probe, amp, mats, to_prev, to_next, have_prev, have_next, window, waves,
+    wave_out, wave_in, top, bottom, pos, counts, pos_prev, pos_next,
+    tile_sem, table_sem, pos_sem, pos_send, pos_recv, win_send, win_recv, wave_send, wave_recv,
     grad_send, grad_recv, own_sem,
 ):
     core = lax.axis_index("depth")
     lat = lax.axis_index("lat")
     has_prev = lat > 0
     has_next = lat < n - 1
-    slots = pos.shape[0]
+    slots = pos.shape[1]
     blocks = tile.shape[0] - 2
     partner = (1 - core, lat)
     sides = ((0, has_prev, (core, lat - 1)), (1, has_next, (core, lat + 1)))
 
+    scalars = [
+        pltpu.make_async_copy(source, target, pos_sem.at[k])
+        for k, (source, target) in enumerate(((pos_hbm, pos), (counts_hbm, counts)))
+    ]
+    for load in scalars:
+        load.start()
     loads = [
         pltpu.make_async_copy(
             trans.at[:, :, :, pl.ds(k * WIN, WIN)], tile.at[k + 1], tile_sem.at[k]
@@ -87,8 +93,12 @@
     ]
     for load in loads:
         load.start()
-    mats_load = pltpu.make_async_copy(mats_hbm, mats, mats_sem)
-    mats_load.start()
+    tables_in = [
+        pltpu.make_async_copy(source, target, table_sem.at[k])
+        for k, (source, target) in enumerate(((mats_hbm, mats), (probe_hbm, probe), (amp_hbm, amp)))
+    ]
+    for load in tables_in:
+        load.start()
 
     barrier = pltpu.get_barrier_semaphore()
     pl.semaphore_signal(barrier, inc=1, device_id=partner, device_id_type=MESH)
@@ -103,30 +113,30 @@
     @pl.when(jnp.logical_not(has_prev))
     def _():
         have_prev[...] = jnp.zeros_like(have_prev)
-        for k in range(4):
-            pos_prev[k, 0] = 0
-            pos_prev[k, 1] = 0
+        for k in range(slots):
+            pos_prev[0, k] = 0
+            pos_prev[1, k] = 0
 
     @pl.when(jnp.logical_not(has_next))
     def _():
         have_next[...] = jnp.zeros_like(have_next)
-        for k in range(4):
-            pos_next[k, 0] = 0
-            pos_next[k, 1] = 0
+        for k in range(slots):
+            pos_next[0, k] = 0
+            pos_next[1, k] = 0
 
     pl.semaphore_wait(barrier, 1 + has_prev.astype(jnp.int32) + has_next.astype(jnp.int32))
 
     def pos_copy(side, device):
         landing = (pos_next, pos_prev)[side]
         return pltpu.make_async_remote_copy(
-            src_ref=pos, dst_ref=landing, send_sem=pos_send.at[side], recv_sem=pos_recv.at[1 - side],
+            src_ref=pos_hbm, dst_ref=landing, send_sem=pos_send.at[side], recv_sem=pos_recv.at[1 - side],
             device_id=device, device_id_type=MESH,
         )
 
     def pos_arrival(side, device):
         landing = (pos_prev, pos_next)[side]
         return pltpu.make_async_remote_copy(
-            src_ref=pos, dst_ref=landing, send_sem=pos_send.at[side], recv_sem=pos_recv.at[side],
+            src_ref=pos_hbm, dst_ref=landing, send_sem=pos_send.at[side], recv_sem=pos_recv.at[side],
             device_id=device, device_id_type=MESH,
         )
 
@@ -178,7 +188,7 @@
         def _():
             pos_copy(side, device).start()
 
-    for load in loads:
+    for load in scalars + loads:
         load.wait()
     for side, there, device in sides:
         @pl.when(there)
@@ -205,7 +215,7 @@
             def _():
                 win_arrival(side, slot, device).wait_recv()
 
-        row = pos[slot, 0] - lat * HALF
+        row = pos[0, slot] - lat * HALF
         rows = lax.broadcasted_iota(jnp.int32, (2, 2, HALF, WIN), 2)
         window[slot, :, :, :HALF] = jnp.where(rows >= row, have_prev[slot], have_next[slot])
         window[slot, :, :, HALF:] = cut(tile, pos, slot)
@@ -235,13 +245,14 @@
 
         own_copy(slot).start()
 
-    mats_load.wait()
+    for load in tables_in:
+        load.wait()
 
     @pl.when(core == 0)
     def _():
         def forward(slot):
             build_window(slot)
-            row = pos[slot, 0] - lat * HALF
+            row = pos[0, slot] - lat * HALF
             _, lane = column_block(pos, slot)
             re = pltpu.roll(pltpu.roll(probe[0], row, 0), lane, 1)
             im = pltpu.roll(pltpu.roll(probe[1], row, 0), lane, 1)
@@ -303,11 +314,11 @@
 
         lax.fori_loop(0, slots, whole, 0)
 
-    for k in range(4):
-        pos_prev_out[k, 0] = pos_prev[k, 0]
-        pos_prev_out[k, 1] = pos_prev[k, 1]
-        pos_next_out[k, 0] = pos_next[k, 0]
-        pos_next_out[k, 1] = pos_next[k, 1]
+    for k in range(slots):
+        for part in range(2):
+            pos_out[0, part, k] = pos[part, k]
+            pos_out[1, part, k] = pos_prev[part, k]
+            pos_out[2, part, k] = pos_next[part, k]
 
     def finish(slot, carry):
         own_copy(slot).wait()
@@ -329,9 +340,10 @@
     lax.fori_loop(0, slots, finish, 0)
 
 
-def place_kernel(n, pos, pos_prev, pos_next, own, from_prev, from_next, out, sums):
+def place_kernel(n, places, own, from_prev, from_next, out, sums):
     lat = lax.axis_index("lat")
     blocks = sums.shape[0] - 2
+    pos, pos_prev, pos_next = places.at[0], places.at[1], places.at[2]
     sums[...] = jnp.zeros_like(sums)
     shape = (2, 2, HALF, WIN)
     rows = lax.broadcasted_iota(jnp.int32, shape, 2)
@@ -349,38 +361,42 @@
 
         @pl.when(lat > 0)
         def _():
-            row = pos_prev[slot, 0] - (lat - 1) * HALF
+            row = pos_prev[0, slot] - (lat - 1) * HALF
             add(pos_prev, slot, from_prev[slot], rows < row)
 
         @pl.when(lat < n - 1)
         def _():
-            row = pos_next[slot, 0] - (lat + 1) * HALF
+            row = pos_next[0, slot] - (lat + 1) * HALF
             add(pos_next, slot, from_next[slot], rows >= row)
 
         return carry
 
-    lax.fori_loop(0, pos.shape[0], one, 0)
+    lax.fori_loop(0, pos.shape[1], one, 0)
     for k in range(blocks):
         out[:, :, :, k * WIN : (k + 1) * WIN] = sums[k + 1]
 
 
 def on_device(n, trans, probe, amp, pos, counts):
     slots = pos.shape[0]
+    pos = pos.T
     blocks = trans.shape[3] // WIN
     smem = pl.BlockSpec(memory_space=pltpu.SMEM)
     vmem = pl.BlockSpec(memory_space=pltpu.VMEM)
-    any_space = pl.BlockSpec(memory_space=pl.ANY)
+    hbm = pl.BlockSpec(memory_space=pltpu.HBM)
     piece = (slots, 2, 2, HALF, WIN)
     wave = (slots, 2, WIN, WIN)
     f32 = jnp.float32
     mats = jnp.asarray(tables())
-    from_prev, from_next, own, pos_prev, pos_next = pl.pallas_call(
+    held = [pltpu.with_memory_space_constraint(x, pltpu.HBM) for x in (pos, trans, probe, amp, mats)]
+    from_prev, from_next, own, places = pl.pallas_call(
         functools.partial(kernel, n),
-        out_shape=[jax.ShapeDtypeStruct(piece, f32)] * 3 + [jax.ShapeDtypeStruct(pos.shape, jnp.int32)] * 2,
-        in_specs=[smem, smem, any_space, vmem, vmem, any_space],
-        out_specs=[any_space, any_space, any_space, smem, smem],
+        out_shape=[pltpu.VMEM(piece, f32)] * 3 + [jax.ShapeDtypeStruct((3, *pos.shape), jnp.int32)],
+        in_specs=[hbm] * 6,
+        out_specs=[vmem, vmem, vmem, smem],
         scratch_shapes=[
             pltpu.VMEM((blocks + 2, 2, 2, HALF, WIN), f32),
+            pltpu.VMEM(probe.shape, f32),
+            pltpu.VMEM(amp.shape, f32),
             pltpu.VMEM(mats.shape, jnp.bfloat16),
             pltpu.VMEM(piece, f32),
             pltpu.VMEM(piece, f32),
@@ -393,9 +409,12 @@
             pltpu.VMEM(piece, f32),
             pltpu.VMEM(piece, f32),
             pltpu.SMEM(pos.shape, jnp.int32),
+            pltpu.SMEM(counts.shape, jnp.int32),
+            pltpu.SMEM(pos.shape, jnp.int32),
             pltpu.SMEM(pos.shape, jnp.int32),
             pltpu.SemaphoreType.DMA((blocks,)),
-            pltpu.SemaphoreType.DMA(()),
+            pltpu.SemaphoreType.DMA((3,)),
+            pltpu.SemaphoreType.DMA((2,)),
             pltpu.SemaphoreType.DMA((2,)),
             pltpu.SemaphoreType.DMA((2,)),
             pltpu.SemaphoreType.DMA((2, slots)),
@@ -410,16 +429,16 @@
             collective_id=0, has_side_effects=True, vmem_limit_bytes=40 << 20
         ),
         name="windows",
-    )(pos, counts, trans, probe, amp, mats)
+    )(held[0], counts, *held[1:])
     return pl.pallas_call(
         functools.partial(place_kernel, n),
         out_shape=jax.ShapeDtypeStruct(trans.shape, f32),
-        in_specs=[smem, smem, smem, vmem, vmem, vmem],
+        in_specs=[smem, vmem, vmem, vmem],
         out_specs=vmem,
         scratch_shapes=[pltpu.VMEM((blocks + 2, 2, 2, HALF, WIN), f32)],
         compiler_params=pltpu.CompilerParams(vmem_limit_bytes=40 << 20),
         name="place",
-    )(pos, pos_prev, pos_next, own, from_prev, from_next)
+    )(places, own, from_prev, from_next)
 
 
 def solution(mesh):

time: 45.9 us -> 41 us (0.89)
  local copies, waits for them, and re-layouts: 4.41 us -> 0 us
    unnamed x11 -> x0, local copies, waits for them, and re-layouts: 4.41 us -> none
where the time goes in v2:
time: 41 us; the launch traced here: 40.8 us
  Pallas kernels  40.2 us (98%)
  between operations  0.66 us (2%)
    pallas_call x1, Pallas kernels, on_device(): pl.pallas_call(functools.partial(kernel, n), out_shape=[pltpu.VMEM(piece,...  38 us
    pallas_call x1, Pallas kernels, on_device(): pl.pallas_call(functools.partial(place_kernel, n), out_shape=jax.ShapeDty...  2.12 us

profile of v2, /device:TPU:96, one launch (start us, length us, event | category | flops | bytes accessed | tf_op | source)
XLA Modules:
  0.0 40.8 jit_solution(7422912144499857123)
XLA Ops:
  0.7 38.0 %windows.1 = (f32[4,2,2,64,128]{4,3,2,1,0:T(8,128)S(1)}, f32[4,2,2,64,128]{4,3,2,1,0:T(8,128)S(1)}, f32[4,2,2,64,128]{4,3,2,1,0:T(8,128)S(1)}, s32[3,2,4]{2,1,0:T(2,128)S(1)}) custom-call(s32[2,4]{1,0:T(2,128)} %bitcast.1, s32[1]{0:T(128)S(6)} %copy.7.counts_hbm, f32[2,2,64,1024]{3,2,1,0:T(8,128)} %trans.1, f32[2,128,128]{2,1,0:T(8,128)} %probe_hbm.1, ...), custom_call_target="tpu_custom_call" | custom-call | tf_op jit(solution)/shard_map/windows/pallas_call | solution.py:391
  38.7 2.1 %place.1 = f32[2,2,64,1024]{3,2,1,0:T(8,128)} custom-call(s32[3,2,4]{2,1,0:T(2,128)S(1)} %get-tuple-element.9.places, f32[4,2,2,64,128]{4,3,2,1,0:T(8,128)S(1)} %get-tuple-element.10.own, f32[4,2,2,64,128]{4,3,2,1,0:T(8,128)S(1)} %get-tuple-element.11.from_prev, f32[4,2,2,64,128]{4,3,2,1,0:T(8,128)S(1)} %get-tuple-element.12.from_next), custom_call_target="tpu_custom_call" | custom-call | tf_op jit(solution)/shard_map/place/pallas_call | solution.py:433

commit v3 on v2

v3 whole, which is shorter than its diff:
```python
import functools

import jax
import jax.numpy as jnp
import ml_dtypes
import numpy as np
from jax import lax
from jax.experimental import pallas as pl
from jax.experimental.pallas import tpu as pltpu
from jax.sharding import PartitionSpec as P

PROP_COEF = 40.0
WIN = 128
HALF = 64
EARLY = 8
MESH = pl.DeviceIdType.MESH
PROP, PROP_CONJ, DFT, DFT_CONJ = range(4)


def tables():
    index = np.arange(WIN)
    dft = np.exp(-2j * np.pi * (np.outer(index, index) % WIN) / WIN) / np.sqrt(WIN)
    freq = ((index + WIN // 2) % WIN - WIN // 2) / WIN
    prop = dft.conj() @ np.diag(np.exp(-1j * PROP_COEF * freq * freq)) @ dft
    terms = []
    for matrix in (prop, prop.conj(), dft, dft.conj()):
        real = np.block([[matrix.real, -matrix.imag], [matrix.imag, matrix.real]])
        high = real.astype(ml_dtypes.bfloat16)
        low = (real - high.astype(np.float64)).astype(ml_dtypes.bfloat16)
        terms.append(np.stack([high, low]))
    return np.stack(terms)


def split(values):
    high = values.astype(jnp.bfloat16)
    low = (values - high.astype(jnp.float32)).astype(jnp.bfloat16)
    return high, low


def product(mats, which, re, im):
    conj = which ^ 1
    high, low = split(jnp.concatenate([re, im], axis=1))
    right = jnp.concatenate([mats[conj, 0], mats[conj, 0], mats[conj, 1]], axis=0)
    first = jnp.dot(
        jnp.concatenate([high, low, high], axis=1), right, preferred_element_type=jnp.float32
    )
    high, low = split(first)
    left = jnp.concatenate(
        [mats[which, 0, :, :WIN], mats[which, 0, :, :WIN], mats[which, 1, :, :WIN]], axis=1
    )
    second = jnp.dot(
        left, jnp.concatenate([high, low, high], axis=0), preferred_element_type=jnp.float32
    )
    return second[:WIN, :WIN] - second[WIN:, WIN:], second[:WIN, WIN:] + second[WIN:, :WIN]


def column_block(pos, slot):
    column = pos[1, slot] + HALF
    return lax.shift_right_logical(column, 7), column & (WIN - 1)


def cut(tile, pos, slot, rows):
    block, lane = column_block(pos, slot)
    first, second = tile[block, :, :, rows], tile[block + 1, :, :, rows]
    lanes = lax.broadcasted_iota(jnp.int32, first.shape, 3)
    return jnp.where(lanes >= lane, first, second)


ALL = slice(0, HALF)
FIRST = slice(0, EARLY)
REST = slice(EARLY, HALF)


def kernel(
    n, pos_hbm, counts_hbm, trans, probe_hbm, amp_hbm, mats_hbm,
    grad,
    tile, probe, amp, mats, full_prev, full_next, to_prev, to_next, to_partner, early_prev, early_next,
    have_prev, have_next, have_own, from_prev, from_next, own, window, waves, top, bottom, pos, counts, pos_prev, pos_next,
    tile_sem, table_sem, pos_sem, pos_send, pos_recv, full_send, full_recv, early_send, early_recv,
    part_send, part_recv, win_send, win_recv, grad_send, grad_recv, bottom_send, bottom_recv,
):
    core = lax.axis_index("depth")
    lat = lax.axis_index("lat")
    has_prev = lat > 0
    has_next = lat < n - 1
    slots = pos.shape[1]
    turns = slots // 2
    blocks = tile.shape[0] - 2
    partner = (1 - core, lat)
    sides = (
        (0, has_prev, lat - 1, pos_prev, full_prev, have_prev, from_prev),
        (1, has_next, lat + 1, pos_next, full_next, have_next, from_next),
    )

    scalars = [
        pltpu.make_async_copy(source, target, pos_sem.at[k])
        for k, (source, target) in enumerate(((pos_hbm, pos), (counts_hbm, counts)))
    ]
    loads = [
        pltpu.make_async_copy(
            trans.at[:, :, :, pl.ds(k * WIN, WIN)], tile.at[k + 1], tile_sem.at[k]
        )
        for k in range(blocks)
    ]
    tables_in = [
        pltpu.make_async_copy(source, target, table_sem.at[k])
        for k, (source, target) in enumerate(((mats_hbm, mats), (probe_hbm, probe), (amp_hbm, amp)))
    ]
    for load in scalars + loads + tables_in:
        load.start()

    barrier = pltpu.get_barrier_semaphore()
    for _, there, place, *_rest in sides:
        @pl.when(there)
        def _():
            for k in (core, 1 - core):
                pl.semaphore_signal(barrier, inc=1, device_id=(k, place), device_id_type=MESH)

    pl.semaphore_signal(barrier, inc=1, device_id=partner, device_id_type=MESH)

    grad[...] = jnp.zeros_like(grad)
    for padded in (tile, full_prev, full_next):
        padded[0] = jnp.zeros(padded.shape[1:], jnp.float32)
        padded[blocks + 1] = jnp.zeros(padded.shape[1:], jnp.float32)
    for _, there, _place, where, full, have, _arrived in sides:
        @pl.when(jnp.logical_not(there))
        def _():
            have[...] = jnp.zeros_like(have)
            for k in range(slots):
                where[0, k] = 0
                where[1, k] = 0

    for load in scalars:
        load.wait()
    pl.semaphore_wait(
        barrier, 1 + 2 * has_prev.astype(jnp.int32) + 2 * has_next.astype(jnp.int32)
    )

    def remote(source, target, send, recv, device):
        return pltpu.make_async_remote_copy(
            src_ref=source, dst_ref=target, send_sem=send, recv_sem=recv,
            device_id=device, device_id_type=MESH,
        )

    def pos_copy(side, place):
        return remote(pos, sides[1 - side][3], pos_send.at[side], pos_recv.at[1 - side], (core, place))

    def pos_arrival(side, place):
        return remote(pos, sides[side][3], pos_send.at[side], pos_recv.at[side], (core, place))

    def full_copy(side, place):
        return remote(
            tile.at[pl.ds(1, blocks), :, :, pl.ds(0, EARLY)], sides[1 - side][4].at[pl.ds(1, blocks)],
            full_send.at[side], full_recv.at[1 - side], (core, place),
        )

    def full_arrival(side, place):
        return remote(
            tile.at[pl.ds(1, blocks), :, :, pl.ds(0, EARLY)], sides[side][4].at[pl.ds(1, blocks)],
            full_send.at[side], full_recv.at[side], (core, place),
        )

    def win_copy(side, turn, to, place):
        slot = 2 * turn + to
        return remote(
            (to_prev, to_next)[side].at[slot], sides[1 - side][5].at[turn, core, :, :, pl.ds(EARLY, HALF - EARLY)],
            win_send.at[side, slot], win_recv.at[1 - side, turn, core], (to, place),
        )

    def win_arrival(side, turn, group, place):
        return remote(
            to_prev.at[0], sides[side][5].at[turn, group, :, :, pl.ds(EARLY, HALF - EARLY)],
            win_send.at[side, 0], win_recv.at[side, turn, group], (core, place),
        )

    def early_copy(side, turn, group):
        return remote(
            (early_prev, early_next)[side].at[turn], sides[side][5].at[turn, group, :, :, pl.ds(0, EARLY)],
            early_send.at[side, turn], early_recv.at[side, turn], partner,
        )

    def part_copy(turn, group):
        return remote(
            to_partner.at[turn], have_own.at[turn, group], part_send.at[turn], part_recv.at[turn], partner
        )

    def grad_copy(side, turn, layer, to, place):
        slot = 2 * turn + core
        return remote(
            top.at[turn, layer], sides[1 - side][6].at[slot, layer % 2],
            grad_send.at[side, turn, layer], grad_recv.at[1 - side, slot, layer % 2], (to, place),
        )

    def grad_arrival(side, slot, part, place):
        return remote(
            top.at[0, 0], sides[side][6].at[slot, part],
            grad_send.at[side, 0, 0], grad_recv.at[side, slot, part], (core, place),
        )

    def bottom_copy(turn, part, slot):
        return remote(
            bottom.at[turn, part], own.at[slot, part], bottom_send.at[turn, part], bottom_recv.at[turn, part], partner
        )

    for side, there, place, *_rest in sides:
        @pl.when(there)
        def _():
            pos_copy(side, place).start()

    for load in loads:
        load.wait()
    for side, there, place, *_rest in sides:
        @pl.when(there)
        def _():
            full_copy(side, place).start()

    def own_windows(turn, carry):
        have_own[turn, core] = cut(tile, pos, 2 * turn + core, ALL)
        to_partner[turn] = cut(tile, pos, 2 * turn + 1 - core, ALL)
        part_copy(turn, core).start()
        return carry

    lax.fori_loop(0, turns, own_windows, 0)

    for side, there, place, *_rest in sides:
        @pl.when(there)
        def _():
            pos_arrival(side, place).wait_recv()

    def send_windows(turn, carry):
        for to in (core, 1 - core):
            slot = 2 * turn + to
            for side, there, place, where, *_rest in sides:
                @pl.when(there)
                def _():
                    (to_prev, to_next)[side][slot] = cut(tile, where, slot, REST)
                    win_copy(side, turn, to, place).start()

        return carry

    lax.fori_loop(0, turns, send_windows, 0)

    def early_windows(turn, carry):
        for side, there, place, _where, full, have, _arrived in sides:
            @pl.when(there)
            def _():
                have[turn, core, :, :, FIRST] = cut(full, pos, 2 * turn + core, FIRST)
                (early_prev, early_next)[side][turn] = cut(full, pos, 2 * turn + 1 - core, FIRST)
                early_copy(side, turn, core).start()

        return carry

    for side, there, place, *_rest in sides:
        @pl.when(there)
        def _():
            full_arrival(side, place).wait_recv()

    lax.fori_loop(0, turns, early_windows, 0)

    for load in tables_in:
        load.wait()

    def build_window(turn, group):
        for side, there, place, *_rest in sides:
            @pl.when(there)
            def _():
                win_arrival(side, turn, group, place).wait_recv()

        @pl.when(core != group)
        def _():
            part_copy(turn, group).wait_recv()
            for side, there, place, *_rest in sides:
                @pl.when(there)
                def _():
                    early_copy(side, turn, group).wait_recv()

        row = pos[0, 2 * turn + core] - lat * HALF
        rows = lax.broadcasted_iota(jnp.int32, (2, 2, HALF, WIN), 2)
        window[group, :, :, :HALF] = jnp.where(rows >= row, have_prev[turn, group], have_next[turn, group])
        window[group, :, :, HALF:] = have_own[turn, group]

    def times(layer, re, im):
        t_re, t_im = window[layer // 2, 0, layer % 2], window[layer // 2, 1, layer % 2]
        return re * t_re - im * t_im, re * t_im + im * t_re

    def times_conj(layer, re, im):
        t_re, t_im = window[layer // 2, 0, layer % 2], window[layer // 2, 1, layer % 2]
        return re * t_re + im * t_im, im * t_re - re * t_im

    def send_term(turn, layer, re, im):
        p_re, p_im = waves[layer, 0], waves[layer, 1]
        term_re = p_re * re + p_im * im
        term_im = p_re * im - p_im * re
        top[turn, layer, 0] = term_re[:HALF]
        top[turn, layer, 1] = term_im[:HALF]
        slot = 2 * turn + core
        group, part = layer // 2, layer % 2
        for at_home, to in ((core == group, core), (core != group, 1 - core)):
            for side, there, place, *_rest in sides:
                @pl.when(jnp.logical_and(there, at_home))
                def _():
                    grad_copy(side, turn, layer, to, place).start()

        @pl.when(core == group)
        def _():
            own[slot, part, 0] = term_re[HALF:]
            own[slot, part, 1] = term_im[HALF:]

        @pl.when(core != group)
        def _():
            bottom[turn, part, 0] = term_re[HALF:]
            bottom[turn, part, 1] = term_im[HALF:]
            bottom_copy(turn, part, slot).start()

    def whole(turn, carry):
        slot = 2 * turn + core
        row = pos[0, slot] - lat * HALF
        _, lane = column_block(pos, slot)
        re = pltpu.roll(pltpu.roll(probe[0], row, 0), lane, 1)
        im = pltpu.roll(pltpu.roll(probe[1], row, 0), lane, 1)
        for layer in range(4):
            if layer % 2 == 0:
                build_window(turn, layer // 2)
            waves[layer, 0] = re
            waves[layer, 1] = im
            re, im = product(mats, PROP if layer < 3 else DFT, *times(layer, re, im))
        live = jnp.where(slot < counts[0], 1.0, 0.0).astype(jnp.float32)
        weight = live * (1.0 - amp[slot] / jnp.sqrt(re * re + im * im + 1.0))
        re, im = product(mats, DFT_CONJ, weight * re, weight * im)
        for layer in range(3, -1, -1):
            send_term(turn, layer, re, im)
            if layer > 0:
                re, im = product(mats, PROP_CONJ, *times_conj(layer, re, im))
        return carry

    lax.fori_loop(0, turns, whole, 0)

    rows = lax.broadcasted_iota(jnp.int32, (2, HALF, WIN), 1)
    lanes = lax.broadcasted_iota(jnp.int32, (2, HALF, WIN), 2)

    def add(where, slot, part, piece):
        begin = where[1, slot] - HALF
        for k in range(blocks):
            offset = lanes + (k * WIN - begin)
            inside = jnp.logical_and(offset >= 0, offset < WIN)
            grad[:, part, :, k * WIN : (k + 1) * WIN] += jnp.where(inside, piece, 0.0)

    def add_own(turn, carry):
        for k in range(2):
            slot = 2 * turn + k
            for part in range(2):
                @pl.when(core != k)
                def _():
                    bottom_copy(turn, part, slot).wait_recv()

                add(pos, slot, part, own[slot, part])
        return carry

    def add_others(slot, carry):
        for part in (1, 0):
            for side, there, place, where, _full, _have, arrived in sides:
                @pl.when(there)
                def _():
                    grad_arrival(side, slot, part, place).wait_recv()
                    row = where[0, slot] - place * HALF
                    keep = rows < row if side == 0 else rows >= row
                    add(where, slot, part, jnp.where(keep, arrived[slot, part], 0.0))

        return carry

    lax.fori_loop(0, turns, add_own, 0)
    lax.fori_loop(0, slots, add_others, 0)

    for side, there, place, *_rest in sides:
        @pl.when(there)
        def _():
            pos_copy(side, place).wait_send()
            full_copy(side, place).wait_send()

    def finish(turn, carry):
        part_copy(turn, core).wait_send()
        for part in range(2):
            bottom_copy(turn, part, 2 * turn + 1 - core).wait_send()
        for side, there, place, *_rest in sides:
            @pl.when(there)
            def _():
                early_copy(side, turn, core).wait_send()
                for layer in range(4):
                    grad_copy(side, turn, layer, core, place).wait_send()
                for to in (core, 1 - core):
                    win_copy(side, turn, to, place).wait_send()

        return carry

    lax.fori_loop(0, turns, finish, 0)


def on_device(n, trans, probe, amp, pos, counts):
    slots = pos.shape[0]
    turns = slots // 2
    pos = pos.T
    blocks = trans.shape[3] // WIN
    vmem = pl.BlockSpec(memory_space=pltpu.VMEM)
    hbm = pl.BlockSpec(memory_space=pltpu.HBM)
    f32 = jnp.float32
    piece = (slots, 2, 2, HALF, WIN)
    mats = jnp.asarray(tables())
    held = [pltpu.with_memory_space_constraint(x, pltpu.HBM) for x in (pos, trans, probe, amp, mats)]
    sem = pltpu.SemaphoreType.DMA
    return pl.pallas_call(
        functools.partial(kernel, n),
        out_shape=pltpu.VMEM(trans.shape, f32),
        in_specs=[hbm] * 6,
        out_specs=vmem,
        scratch_shapes=[
            pltpu.VMEM((blocks + 2, 2, 2, HALF, WIN), f32),
            pltpu.VMEM(probe.shape, f32),
            pltpu.VMEM(amp.shape, f32),
            pltpu.VMEM(mats.shape, jnp.bfloat16),
            pltpu.VMEM((blocks + 2, 2, 2, EARLY, WIN), f32),
            pltpu.VMEM((blocks + 2, 2, 2, EARLY, WIN), f32),
            pltpu.VMEM((slots, 2, 2, HALF - EARLY, WIN), f32),
            pltpu.VMEM((slots, 2, 2, HALF - EARLY, WIN), f32),
            pltpu.VMEM((turns, 2, 2, HALF, WIN), f32),
            pltpu.VMEM((turns, 2, 2, EARLY, WIN), f32),
            pltpu.VMEM((turns, 2, 2, EARLY, WIN), f32),
            pltpu.VMEM((turns, 2, 2, 2, HALF, WIN), f32),
            pltpu.VMEM((turns, 2, 2, 2, HALF, WIN), f32),
            pltpu.VMEM((turns, 2, 2, 2, HALF, WIN), f32),
            pltpu.VMEM(piece, f32),
            pltpu.VMEM(piece, f32),
            pltpu.VMEM(piece, f32),
            pltpu.VMEM((2, 2, 2, WIN, WIN), f32),
            pltpu.VMEM((4, 2, WIN, WIN), f32),
            pltpu.VMEM((turns, 4, 2, HALF, WIN), f32),
            pltpu.VMEM((turns, 2, 2, HALF, WIN), f32),
            pltpu.SMEM(pos.shape, jnp.int32),
            pltpu.SMEM(counts.shape, jnp.int32),
            pltpu.SMEM(pos.shape, jnp.int32),
            pltpu.SMEM(pos.shape, jnp.int32),
            sem((blocks,)),
            sem((3,)),
            sem((2,)),
            sem((2,)),
            sem((2,)),
            sem((2,)),
            sem((2,)),
            sem((2, turns)),
            sem((2, turns)),
            sem((turns,)),
            sem((turns,)),
            sem((2, slots)),
            sem((2, turns, 2)),
            sem((2, turns, 4)),
            sem((2, slots, 2)),
            sem((turns, 2)),
            sem((turns, 2)),
        ],
        compiler_params=pltpu.CompilerParams(
            collective_id=0, has_side_effects=True, vmem_limit_bytes=40 << 20
        ),
        name="windows",
    )(held[0], counts, *held[1:])


def solution(mesh):
    placed = (P(None, "depth", "lat", None), P(), P("lat", None, None), P("lat", None), P("lat"))
    return jax.shard_map(
        functools.partial(on_device, mesh.shape["lat"]),
        mesh=mesh,
        in_specs=placed,
        out_specs=P(None, "depth", "lat", None),
        check_vma=False,
    )
```

time: 41 us -> 36.6 us (0.89)
  Pallas kernels: 40.2 us -> 34.8 us
  local copies, waits for them, and re-layouts: 0 us -> 0.97 us
    pallas_call x2 -> x1, Pallas kernels: 40.2 us -> 34.8 us  [on_device(): pl.pallas_call(functools.partial(kernel, n), out_shape=pltpu.VMEM(trans.s...]
    unnamed x0 -> x1, local copies, waits for them, and re-layouts: none -> 0.97 us
where the time goes in v3:
time: 36.6 us; the launch traced here: 36.4 us
  Pallas kernels  34.8 us (95%)
  local copies, waits for them, and re-layouts  0.97 us (3%)
  between operations  0.66 us (2%)
    pallas_call x1, Pallas kernels, on_device(): pl.pallas_call(functools.partial(kernel, n), out_shape=pltpu.VMEM(trans.s...  34.8 us
    unnamed x1, local copies, waits for them, and re-layouts  0.97 us

profile of v3, /device:TPU:96, one launch (start us, length us, event | category | flops | bytes accessed | tf_op | source)
XLA Modules:
  0.0 36.4 jit_solution(6274761679582336016)
XLA Ops:
  0.7 34.8 %windows.1 = f32[2,2,64,1024]{3,2,1,0:T(8,128)S(1)} custom-call(s32[2,4]{1,0:T(2,128)} %bitcast.1, s32[1]{0:T(128)S(6)} %copy.9.counts_hbm, f32[2,2,64,1024]{3,2,1,0:T(8,128)} %trans.1, f32[2,128,128]{2,1,0:T(8,128)} %probe_hbm.1, f32[4,128,128]{2,1,0:T(8,128)} %amp_hbm.1, bf16[4,2,256,256]{3,2,1,0:T(8,128)(2,1)} %constant.2.clone.mats_hbm), custom_call_target="tpu_custom_call" | custom-call | tf_op jit(solution)/shard_map/windows/pallas_call | solution.py:410
  35.4 1.0 %copy.8 = f32[2,2,64,1024]{3,2,1,0:T(8,128)} copy(f32[2,2,64,1024]{3,2,1,0:T(8,128)S(1)} %windows.1) | data formatting | bytes 2097152

commit v4 on v3

--- a/solution.py
+++ b/solution.py
@@ -13,6 +13,8 @@
 WIN = 128
 HALF = 64
 EARLY = 8
+PLANE = 16
+DETOUR = 3
 MESH = pl.DeviceIdType.MESH
 PROP, PROP_CONJ, DFT, DFT_CONJ = range(4)
 
@@ -66,23 +68,32 @@
     return jnp.where(lanes >= lane, first, second)
 
 
+DETOURED = (3, 2)
 ALL = slice(0, HALF)
 FIRST = slice(0, EARLY)
+SECOND = slice(EARLY, 2 * EARLY)
 REST = slice(EARLY, HALF)
 
 
 def kernel(
     n, pos_hbm, counts_hbm, trans, probe_hbm, amp_hbm, mats_hbm,
     grad,
-    tile, probe, amp, mats, full_prev, full_next, to_prev, to_next, to_partner, early_prev, early_next,
-    have_prev, have_next, have_own, from_prev, from_next, own, window, waves, top, bottom, pos, counts, pos_prev, pos_next,
-    tile_sem, table_sem, pos_sem, pos_send, pos_recv, full_send, full_recv, early_send, early_recv,
-    part_send, part_recv, win_send, win_recv, grad_send, grad_recv, bottom_send, bottom_recv,
+    tile, probe, amp, mats, full_prev, full_next, more_prev, to_prev, to_next, to_partner, early_prev, early_next, early_more,
+    have_prev, have_next, have_own, from_prev, from_next, own, window, waves, top, bottom, passed, pos, counts, pos_prev, pos_next, pos_pass,
+    here_sem, tile_sem, table_sem, pos_sem, pos_send, pos_recv, full_send, full_recv, early_send, early_recv,
+    more_send, more_recv, extra_send, extra_recv,
+    part_send, part_recv, win_send, win_recv, grad_send, grad_recv, bottom_send, bottom_recv, passed_send, passed_recv, pass_send, pass_recv,
 ):
     core = lax.axis_index("depth")
     lat = lax.axis_index("lat")
     has_prev = lat > 0
     has_next = lat < n - 1
+    far_prev = jnp.logical_and(has_prev, lax.rem(lat, PLANE) == 0)
+    far_next = jnp.logical_and(has_next, lax.rem(lat, PLANE) == PLANE - 1)
+    first_of_plane, last_of_plane = lat - DETOUR, lat + DETOUR
+    passes_up = jnp.logical_and(first_of_plane > 0, lax.rem(first_of_plane, PLANE) == 0)
+    passes_down = jnp.logical_and(last_of_plane < n - 1, lax.rem(last_of_plane, PLANE) == PLANE - 1)
+    passes = jnp.logical_or(passes_up, passes_down)
     slots = pos.shape[1]
     turns = slots // 2
     blocks = tile.shape[0] - 2
@@ -110,16 +121,39 @@
         load.start()
 
     barrier = pltpu.get_barrier_semaphore()
-    for _, there, place, *_rest in sides:
-        @pl.when(there)
+    near_prev = jnp.logical_and(has_prev, jnp.logical_not(far_prev))
+    near_next = jnp.logical_and(has_next, jnp.logical_not(far_next))
+    first, second = core == 0, core == 1
+    to_same = ((has_prev, lat - 1), (jnp.logical_or(near_next, jnp.logical_and(far_next, first)), lat + 1))
+    to_other = ((has_prev, lat - 1), (jnp.logical_or(near_next, jnp.logical_and(far_next, second)), lat + 1))
+    for targets, k in ((to_same, core), (to_other, 1 - core)):
+        for there, place in targets:
+            @pl.when(there)
+            def _():
+                pl.semaphore_signal(barrier, inc=1, device_id=(k, place), device_id_type=MESH)
+
+    pl.semaphore_signal(barrier, inc=1, device_id=partner, device_id_type=MESH)
+
+    @pl.when(passes_up)
+    def _():
+        pl.semaphore_signal(barrier, inc=1, device_id=(core, lat - DETOUR - 1), device_id_type=MESH)
+
+    @pl.when(passes_down)
+    def _():
+        pl.semaphore_signal(barrier, inc=1, device_id=(core, lat + DETOUR + 1), device_id_type=MESH)
+
+    @pl.when(jnp.logical_and(far_next, first))
+    def _():
+        pl.semaphore_signal(barrier, inc=1, device_id=(1 - core, lat - DETOUR), device_id_type=MESH)
+
+    for flag, place in ((far_prev, lat + DETOUR), (far_next, lat - DETOUR)):
+        @pl.when(jnp.logical_and(flag, core == 1))
         def _():
             for k in (core, 1 - core):
                 pl.semaphore_signal(barrier, inc=1, device_id=(k, place), device_id_type=MESH)
 
-    pl.semaphore_signal(barrier, inc=1, device_id=partner, device_id_type=MESH)
-
     grad[...] = jnp.zeros_like(grad)
-    for padded in (tile, full_prev, full_next):
+    for padded in (tile, full_prev, full_next, more_prev):
         padded[0] = jnp.zeros(padded.shape[1:], jnp.float32)
         padded[blocks + 1] = jnp.zeros(padded.shape[1:], jnp.float32)
     for _, there, _place, where, full, have, _arrived in sides:
@@ -133,7 +167,10 @@
     for load in scalars:
         load.wait()
     pl.semaphore_wait(
-        barrier, 1 + 2 * has_prev.astype(jnp.int32) + 2 * has_next.astype(jnp.int32)
+        barrier,
+        1 + 2 * jnp.logical_or(near_prev, jnp.logical_and(far_prev, first)).astype(jnp.int32)
+        + 2 * has_next.astype(jnp.int32) + jnp.logical_and(passes_down, second).astype(jnp.int32)
+        + far_prev.astype(jnp.int32) + far_next.astype(jnp.int32) + passes.astype(jnp.int32),
     )
 
     def remote(source, target, send, recv, device):
@@ -160,17 +197,44 @@
             full_send.at[side], full_recv.at[side], (core, place),
         )
 
-    def win_copy(side, turn, to, place):
-        slot = 2 * turn + to
-        return remote(
-            (to_prev, to_next)[side].at[slot], sides[1 - side][5].at[turn, core, :, :, pl.ds(EARLY, HALF - EARLY)],
+    def more_copy():
+        return remote(
+            tile.at[pl.ds(1, blocks), :, :, pl.ds(EARLY, EARLY)], more_prev.at[pl.ds(1, blocks)],
+            more_send, more_recv, (core, lat + 1),
+        )
+
+    def more_arrival():
+        return remote(
+            tile.at[pl.ds(1, blocks), :, :, pl.ds(EARLY, EARLY)], more_prev.at[pl.ds(1, blocks)],
+            more_send, more_recv, (core, lat - 1),
+        )
+
+    def when_near_or_far(side, there, far, act):
+        if side == 0:
+            pl.when(there)(functools.partial(act, EARLY))
+        else:
+            pl.when(jnp.logical_and(there, jnp.logical_not(far)))(functools.partial(act, EARLY))
+            pl.when(jnp.logical_and(there, far))(functools.partial(act, 2 * EARLY))
+
+    def win_copy(side, turn, to, place, begin):
+        slot, rows = 2 * turn + to, HALF - begin
+        return remote(
+            (to_prev, to_next)[side].at[slot, :, :, pl.ds(begin - EARLY, rows)],
+            sides[1 - side][5].at[turn, core, :, :, pl.ds(begin, rows)],
             win_send.at[side, slot], win_recv.at[1 - side, turn, core], (to, place),
         )
 
-    def win_arrival(side, turn, group, place):
-        return remote(
-            to_prev.at[0], sides[side][5].at[turn, group, :, :, pl.ds(EARLY, HALF - EARLY)],
+    def win_arrival(side, turn, group, place, begin):
+        rows = HALF - begin
+        return remote(
+            to_prev.at[0, :, :, pl.ds(begin - EARLY, rows)], sides[side][5].at[turn, group, :, :, pl.ds(begin, rows)],
             win_send.at[side, 0], win_recv.at[side, turn, group], (core, place),
+        )
+
+    def extra_copy(turn, group):
+        return remote(
+            early_more.at[turn], have_prev.at[turn, group, :, :, pl.ds(EARLY, EARLY)],
+            extra_send.at[turn], extra_recv.at[turn], partner,
         )
 
     def early_copy(side, turn, group):
@@ -197,22 +261,65 @@
             grad_send.at[side, 0, 0], grad_recv.at[side, slot, part], (core, place),
         )
 
+    def detour_copy(side, turn, layer):
+        return remote(
+            top.at[turn, layer], passed.at[layer % 2], grad_send.at[side, turn, layer], passed_recv.at[layer % 2],
+            (core, lat + (DETOUR + 1 if side else -DETOUR - 1)),
+        )
+
+    def passed_copy(side, part):
+        to, place = (1 - core, lat - DETOUR) if side == 0 else (1 - core, lat + DETOUR)
+        return [
+            remote(
+                passed.at[part], sides[side][6].at[core, part], passed_send.at[part], grad_recv.at[side, core, part],
+                (k, place),
+            )
+            for k in (core, to)
+        ]
+
     def bottom_copy(turn, part, slot):
         return remote(
             bottom.at[turn, part], own.at[slot, part], bottom_send.at[turn, part], bottom_recv.at[turn, part], partner
         )
+
+    def pos_pass_copy():
+        return remote(pos, pos_pass, pass_send.at[0], pass_recv, (core, lat - DETOUR - 1))
+
+    def pos_passed_copies():
+        return [
+            remote(pos_pass, pos_next, pass_send.at[i], pos_recv.at[1], (k, lat + DETOUR))
+            for i, k in enumerate((core, 1 - core))
+        ]
+
+    @pl.when(jnp.logical_and(far_prev, first))
+    def _():
+        pl.semaphore_signal(here_sem, inc=1, device_id=partner, device_id_type=MESH)
+
+    @pl.when(jnp.logical_and(far_prev, second))
+    def _():
+        pos_pass_copy().start()
+
+    tells = (near_prev, has_next)
+    for side, _there, place, *_rest in sides:
+        @pl.when(tells[side])
+        def _():
+            pos_copy(side, place).start()
+
+    for load in loads:
+        load.wait()
+
+    @pl.when(jnp.logical_and(far_prev, second))
+    def _():
+        pl.semaphore_wait(here_sem, 1)
 
     for side, there, place, *_rest in sides:
         @pl.when(there)
         def _():
-            pos_copy(side, place).start()
-
-    for load in loads:
-        load.wait()
-    for side, there, place, *_rest in sides:
-        @pl.when(there)
-        def _():
             full_copy(side, place).start()
+
+    @pl.when(far_next)
+    def _():
+        more_copy().start()
 
     def own_windows(turn, carry):
         have_own[turn, core] = cut(tile, pos, 2 * turn + core, ALL)
@@ -227,14 +334,25 @@
         def _():
             pos_arrival(side, place).wait_recv()
 
+    @pl.when(jnp.logical_and(passes_down, second))
+    def _():
+        pos_pass_copy().wait_recv()
+        for copy in pos_passed_copies():
+            copy.start()
+
     def send_windows(turn, carry):
-        for to in (core, 1 - core):
-            slot = 2 * turn + to
+        for k in range(2):
+            slot = 2 * turn + k
             for side, there, place, where, *_rest in sides:
                 @pl.when(there)
                 def _():
                     (to_prev, to_next)[side][slot] = cut(tile, where, slot, REST)
-                    win_copy(side, turn, to, place).start()
+
+                for at_home, to in ((core == k, core), (core != k, 1 - core)):
+                    when_near_or_far(
+                        side, jnp.logical_and(there, at_home), far_next,
+                        lambda begin: win_copy(side, turn, to, place, begin).start(),
+                    )
 
         return carry
 
@@ -257,14 +375,26 @@
 
     lax.fori_loop(0, turns, early_windows, 0)
 
+    @pl.when(far_prev)
+    def _():
+        more_arrival().wait_recv()
+
+        def extra_windows(turn, carry):
+            have_prev[turn, core, :, :, SECOND] = cut(more_prev, pos, 2 * turn + core, FIRST)
+            early_more[turn] = cut(more_prev, pos, 2 * turn + 1 - core, FIRST)
+            extra_copy(turn, core).start()
+            return carry
+
+        lax.fori_loop(0, turns, extra_windows, 0)
+
     for load in tables_in:
         load.wait()
 
     def build_window(turn, group):
         for side, there, place, *_rest in sides:
-            @pl.when(there)
-            def _():
-                win_arrival(side, turn, group, place).wait_recv()
+            when_near_or_far(
+                1 - side, there, far_prev, lambda begin: win_arrival(side, turn, group, place, begin).wait_recv()
+            )
 
         @pl.when(core != group)
         def _():
@@ -273,6 +403,10 @@
                 @pl.when(there)
                 def _():
                     early_copy(side, turn, group).wait_recv()
+
+            @pl.when(far_prev)
+            def _():
+                extra_copy(turn, group).wait_recv()
 
         row = pos[0, 2 * turn + core] - lat * HALF
         rows = lax.broadcasted_iota(jnp.int32, (2, 2, HALF, WIN), 2)
@@ -297,7 +431,17 @@
         group, part = layer // 2, layer % 2
         for at_home, to in ((core == group, core), (core != group, 1 - core)):
             for side, there, place, *_rest in sides:
-                @pl.when(jnp.logical_and(there, at_home))
+                goes = jnp.logical_and(there, at_home)
+                if layer in DETOURED:
+                    around = jnp.logical_and((far_prev, far_next)[side], turn == 0)
+
+                    @pl.when(jnp.logical_and(goes, around))
+                    def _():
+                        detour_copy(side, turn, layer).start()
+
+                    goes = jnp.logical_and(goes, jnp.logical_not(around))
+
+                @pl.when(goes)
                 def _():
                     grad_copy(side, turn, layer, to, place).start()
 
@@ -335,6 +479,25 @@
 
     lax.fori_loop(0, turns, whole, 0)
 
+    for side, flag in ((0, passes_up), (1, passes_down)):
+        for part in [layer % 2 for layer in DETOURED]:
+            @pl.when(flag)
+            def _():
+                pltpu.make_async_remote_copy(
+                    src_ref=top.at[0, 0], dst_ref=passed.at[part], send_sem=grad_send.at[side, 0, 0],
+                    recv_sem=passed_recv.at[part], device_id=partner, device_id_type=MESH,
+                ).wait_recv()
+
+            same, other = passed_copy(side, part)
+
+            @pl.when(jnp.logical_and(flag, core == 1))
+            def _():
+                same.start()
+
+            @pl.when(jnp.logical_and(flag, core == 0))
+            def _():
+                other.start()
+
     rows = lax.broadcasted_iota(jnp.int32, (2, HALF, WIN), 1)
     lanes = lax.broadcasted_iota(jnp.int32, (2, HALF, WIN), 2)
 
@@ -356,26 +519,59 @@
                 add(pos, slot, part, own[slot, part])
         return carry
 
+    def add_other(slot, part, side, when):
+        _, _there, place, where, _full, _have, arrived = sides[side]
+
+        @pl.when(when)
+        def _():
+            grad_arrival(side, slot, part, place).wait_recv()
+            row = where[0, slot] - place * HALF
+            keep = rows < row if side == 0 else rows >= row
+            add(where, slot, part, jnp.where(keep, arrived[slot, part], 0.0))
+
+    detoured = [layer % 2 for layer in DETOURED]
+    by_detour = [jnp.logical_and(flag, core == 1) for flag in (far_prev, far_next)]
+
     def add_others(slot, carry):
         for part in (1, 0):
-            for side, there, place, where, _full, _have, arrived in sides:
-                @pl.when(there)
-                def _():
-                    grad_arrival(side, slot, part, place).wait_recv()
-                    row = where[0, slot] - place * HALF
-                    keep = rows < row if side == 0 else rows >= row
-                    add(where, slot, part, jnp.where(keep, arrived[slot, part], 0.0))
-
+            for side, there, *_rest in sides:
+                if part in detoured:
+                    there = jnp.logical_and(there, jnp.logical_not(jnp.logical_and(by_detour[side], slot < 2)))
+                add_other(slot, part, side, there)
+        return carry
+
+    def add_detoured(slot, carry):
+        for part in detoured:
+            for side in range(2):
+                add_other(slot, part, side, by_detour[side])
         return carry
 
     lax.fori_loop(0, turns, add_own, 0)
     lax.fori_loop(0, slots, add_others, 0)
+    if DETOURED:
+        lax.fori_loop(0, 2, add_detoured, 0)
 
     for side, there, place, *_rest in sides:
         @pl.when(there)
         def _():
+            full_copy(side, place).wait_send()
+
+        @pl.when(tells[side])
+        def _():
             pos_copy(side, place).wait_send()
-            full_copy(side, place).wait_send()
+
+    @pl.when(jnp.logical_and(far_prev, second))
+    def _():
+        pos_pass_copy().wait_send()
+
+    @pl.when(jnp.logical_and(passes_down, second))
+    def _():
+        for copy in pos_passed_copies():
+            copy.wait_send()
+
+    @pl.when(far_next)
+    def _():
+        more_copy().wait_send()
 
     def finish(turn, carry):
         part_copy(turn, core).wait_send()
@@ -387,12 +583,24 @@
                 early_copy(side, turn, core).wait_send()
                 for layer in range(4):
                     grad_copy(side, turn, layer, core, place).wait_send()
-                for to in (core, 1 - core):
-                    win_copy(side, turn, to, place).wait_send()
+
+            for to in (core, 1 - core):
+                when_near_or_far(
+                    side, there, far_next, lambda begin: win_copy(side, turn, to, place, begin).wait_send()
+                )
+
+        @pl.when(far_prev)
+        def _():
+            extra_copy(turn, core).wait_send()
 
         return carry
 
     lax.fori_loop(0, turns, finish, 0)
+
+    @pl.when(passes)
+    def _():
+        for layer in DETOURED:
+            passed_copy(0, layer % 2)[0].wait_send()
 
 
 def on_device(n, trans, probe, amp, pos, counts):
@@ -419,9 +627,11 @@
             pltpu.VMEM(mats.shape, jnp.bfloat16),
             pltpu.VMEM((blocks + 2, 2, 2, EARLY, WIN), f32),
             pltpu.VMEM((blocks + 2, 2, 2, EARLY, WIN), f32),
+            pltpu.VMEM((blocks + 2, 2, 2, EARLY, WIN), f32),
             pltpu.VMEM((slots, 2, 2, HALF - EARLY, WIN), f32),
             pltpu.VMEM((slots, 2, 2, HALF - EARLY, WIN), f32),
             pltpu.VMEM((turns, 2, 2, HALF, WIN), f32),
+            pltpu.VMEM((turns, 2, 2, EARLY, WIN), f32),
             pltpu.VMEM((turns, 2, 2, EARLY, WIN), f32),
             pltpu.VMEM((turns, 2, 2, EARLY, WIN), f32),
             pltpu.VMEM((turns, 2, 2, 2, HALF, WIN), f32),
@@ -434,10 +644,13 @@
             pltpu.VMEM((4, 2, WIN, WIN), f32),
             pltpu.VMEM((turns, 4, 2, HALF, WIN), f32),
             pltpu.VMEM((turns, 2, 2, HALF, WIN), f32),
+            pltpu.VMEM((2, 2, HALF, WIN), f32),
             pltpu.SMEM(pos.shape, jnp.int32),
             pltpu.SMEM(counts.shape, jnp.int32),
             pltpu.SMEM(pos.shape, jnp.int32),
             pltpu.SMEM(pos.shape, jnp.int32),
+            pltpu.SMEM(pos.shape, jnp.int32),
+            pltpu.SemaphoreType.REGULAR,
             sem((blocks,)),
             sem((3,)),
             sem((2,)),
@@ -447,6 +660,10 @@
             sem((2,)),
             sem((2, turns)),
             sem((2, turns)),
+            sem(()),
+            sem(()),
+            sem((turns,)),
+            sem((turns,)),
             sem((turns,)),
             sem((turns,)),
             sem((2, slots)),
@@ -455,6 +672,10 @@
             sem((2, slots, 2)),
             sem((turns, 2)),
             sem((turns, 2)),
+            sem((2,)),
+            sem((2,)),
+            sem((2,)),
+            sem(()),
         ],
         compiler_params=pltpu.CompilerParams(
             collective_id=0, has_side_effects=True, vmem_limit_bytes=40 << 20

time: 36.6 us -> 36.3 us (level)
  no operation moved by 1% of the time
where the time goes in v4:
time: 36.3 us; the launch traced here: 36.1 us
  Pallas kernels  34.5 us (95%)
  local copies, waits for them, and re-layouts  0.97 us (3%)
  between operations  0.66 us (2%)
    pallas_call x1, Pallas kernels, on_device(): pl.pallas_call(functools.partial(kernel, n), out_shape=pltpu.VMEM(trans.s...  34.5 us
    unnamed x1, local copies, waits for them, and re-layouts  0.97 us

profile of v4, /device:TPU:96, one launch (start us, length us, event | category | flops | bytes accessed | tf_op | source)
XLA Modules:
  0.0 36.1 jit_solution(14933566058948094812)
XLA Ops:
  0.7 34.5 %windows.1 = f32[2,2,64,1024]{3,2,1,0:T(8,128)S(1)} custom-call(s32[2,4]{1,0:T(2,128)} %bitcast.1, s32[1]{0:T(128)S(6)} %copy.9.counts_hbm, f32[2,2,64,1024]{3,2,1,0:T(8,128)} %trans.1, f32[2,128,128]{2,1,0:T(8,128)} %probe_hbm.1, f32[4,128,128]{2,1,0:T(8,128)} %amp_hbm.1, bf16[4,2,256,256]{3,2,1,0:T(8,128)(2,1)} %constant.2.clone.mats_hbm), custom_call_target="tpu_custom_call" | custom-call | tf_op jit(solution)/shard_map/windows/pallas_call | solution.py:618
  35.2 1.0 %copy.8 = f32[2,2,64,1024]{3,2,1,0:T(8,128)} copy(f32[2,2,64,1024]{3,2,1,0:T(8,128)S(1)} %windows.1) | data formatting | bytes 2097152

commit v5 on v4

--- a/solution.py
+++ b/solution.py
@@ -68,7 +68,7 @@
     return jnp.where(lanes >= lane, first, second)
 
 
-DETOURED = (3, 2)
+DETOURED = (3,)
 ALL = slice(0, HALF)
 FIRST = slice(0, EARLY)
 SECOND = slice(EARLY, 2 * EARLY)
@@ -271,7 +271,7 @@
         to, place = (1 - core, lat - DETOUR) if side == 0 else (1 - core, lat + DETOUR)
         return [
             remote(
-                passed.at[part], sides[side][6].at[core, part], passed_send.at[part], grad_recv.at[side, core, part],
+                passed.at[part], sides[side][6].at[2 + core, part], passed_send.at[part], grad_recv.at[side, 2 + core, part],
                 (k, place),
             )
             for k in (core, to)
@@ -433,7 +433,7 @@
             for side, there, place, *_rest in sides:
                 goes = jnp.logical_and(there, at_home)
                 if layer in DETOURED:
-                    around = jnp.logical_and((far_prev, far_next)[side], turn == 0)
+                    around = jnp.logical_and((far_prev, far_next)[side], turn == 1)
 
                     @pl.when(jnp.logical_and(goes, around))
                     def _():
@@ -479,6 +479,57 @@
 
     lax.fori_loop(0, turns, whole, 0)
 
+    rows = lax.broadcasted_iota(jnp.int32, (2, HALF, WIN), 1)
+    lanes = lax.broadcasted_iota(jnp.int32, (2, HALF, WIN), 2)
+
+    def add(where, slot, part, piece):
+        begin = where[1, slot] - HALF
+        for k in range(blocks):
+            offset = lanes + (k * WIN - begin)
+            inside = jnp.logical_and(offset >= 0, offset < WIN)
+            grad[:, part, :, k * WIN : (k + 1) * WIN] += jnp.where(inside, piece, 0.0)
+
+    def add_own(turn, carry):
+        for k in range(2):
+            slot = 2 * turn + k
+            for part in range(2):
+                @pl.when(core != k)
+                def _():
+                    bottom_copy(turn, part, slot).wait_recv()
+
+                add(pos, slot, part, own[slot, part])
+        return carry
+
+    def add_other(slot, part, side, when):
+        _, _there, place, where, _full, _have, arrived = sides[side]
+
+        @pl.when(when)
+        def _():
+            grad_arrival(side, slot, part, place).wait_recv()
+            row = where[0, slot] - place * HALF
+            keep = rows < row if side == 0 else rows >= row
+            add(where, slot, part, jnp.where(keep, arrived[slot, part], 0.0))
+
+    detoured = [layer % 2 for layer in DETOURED]
+    by_detour = [jnp.logical_and(flag, core == 1) for flag in (far_prev, far_next)]
+
+    def add_others(slot, carry):
+        for part in (1, 0):
+            for side, there, *_rest in sides:
+                if part in detoured:
+                    there = jnp.logical_and(there, jnp.logical_not(jnp.logical_and(by_detour[side], slot >= 2)))
+                add_other(slot, part, side, there)
+        return carry
+
+    def add_detoured(slot, carry):
+        for part in detoured:
+            for side in range(2):
+                add_other(slot, part, side, by_detour[side])
+        return carry
+
+    lax.fori_loop(0, turns, add_own, 0)
+    lax.fori_loop(0, 2, add_others, 0)
+
     for side, flag in ((0, passes_up), (1, passes_down)):
         for part in [layer % 2 for layer in DETOURED]:
             @pl.when(flag)
@@ -498,58 +549,9 @@
             def _():
                 other.start()
 
-    rows = lax.broadcasted_iota(jnp.int32, (2, HALF, WIN), 1)
-    lanes = lax.broadcasted_iota(jnp.int32, (2, HALF, WIN), 2)
-
-    def add(where, slot, part, piece):
-        begin = where[1, slot] - HALF
-        for k in range(blocks):
-            offset = lanes + (k * WIN - begin)
-            inside = jnp.logical_and(offset >= 0, offset < WIN)
-            grad[:, part, :, k * WIN : (k + 1) * WIN] += jnp.where(inside, piece, 0.0)
-
-    def add_own(turn, carry):
-        for k in range(2):
-            slot = 2 * turn + k
-            for part in range(2):
-                @pl.when(core != k)
-                def _():
-                    bottom_copy(turn, part, slot).wait_recv()
-
-                add(pos, slot, part, own[slot, part])
-        return carry
-
-    def add_other(slot, part, side, when):
-        _, _there, place, where, _full, _have, arrived = sides[side]
-
-        @pl.when(when)
-        def _():
-            grad_arrival(side, slot, part, place).wait_recv()
-            row = where[0, slot] - place * HALF
-            keep = rows < row if side == 0 else rows >= row
-            add(where, slot, part, jnp.where(keep, arrived[slot, part], 0.0))
-
-    detoured = [layer % 2 for layer in DETOURED]
-    by_detour = [jnp.logical_and(flag, core == 1) for flag in (far_prev, far_next)]
-
-    def add_others(slot, carry):
-        for part in (1, 0):
-            for side, there, *_rest in sides:
-                if part in detoured:
-                    there = jnp.logical_and(there, jnp.logical_not(jnp.logical_and(by_detour[side], slot < 2)))
-                add_other(slot, part, side, there)
-        return carry
-
-    def add_detoured(slot, carry):
-        for part in detoured:
-            for side in range(2):
-                add_other(slot, part, side, by_detour[side])
-        return carry
-
-    lax.fori_loop(0, turns, add_own, 0)
-    lax.fori_loop(0, slots, add_others, 0)
+    lax.fori_loop(2, slots, add_others, 0)
     if DETOURED:
-        lax.fori_loop(0, 2, add_detoured, 0)
+        lax.fori_loop(2, slots, add_detoured, 0)
 
     for side, there, place, *_rest in sides:
         @pl.when(there)

time: 36.3 us -> 35.5 us (0.978)
  Pallas kernels: 34.5 us -> 33.8 us
    pallas_call x1, Pallas kernels: 34.5 us -> 33.8 us  [on_device(): pl.pallas_call(functools.partial(kernel, n), out_shape=pltpu.VMEM(trans.s...]
where the time goes in v5:
time: 35.5 us; the launch traced here: 35.4 us
  Pallas kernels  33.8 us (95%)
  local copies, waits for them, and re-layouts  0.97 us (3%)
  between operations  0.66 us (2%)
    pallas_call x1, Pallas kernels, on_device(): pl.pallas_call(functools.partial(kernel, n), out_shape=pltpu.VMEM(trans.s...  33.8 us
    unnamed x1, local copies, waits for them, and re-layouts  0.97 us

profile of v5, /device:TPU:96, one launch (start us, length us, event | category | flops | bytes accessed | tf_op | source)
XLA Modules:
  0.0 35.4 jit_solution(637906204617165491)
XLA Ops:
  0.7 33.8 %windows.1 = f32[2,2,64,1024]{3,2,1,0:T(8,128)S(1)} custom-call(s32[2,4]{1,0:T(2,128)} %bitcast.1, s32[1]{0:T(128)S(6)} %copy.9.counts_hbm, f32[2,2,64,1024]{3,2,1,0:T(8,128)} %trans.1, f32[2,128,128]{2,1,0:T(8,128)} %probe_hbm.1, f32[4,128,128]{2,1,0:T(8,128)} %amp_hbm.1, bf16[4,2,256,256]{3,2,1,0:T(8,128)(2,1)} %constant.2.clone.mats_hbm), custom_call_target="tpu_custom_call" | custom-call | tf_op jit(solution)/shard_map/windows/pallas_call | solution.py:620
  34.4 1.0 %copy.8 = f32[2,2,64,1024]{3,2,1,0:T(8,128)} copy(f32[2,2,64,1024]{3,2,1,0:T(8,128)S(1)} %windows.1) | data formatting | bytes 2097152

commit v6 on v5

--- a/solution.py
+++ b/solution.py
@@ -549,7 +549,19 @@
             def _():
                 other.start()
 
-    lax.fori_loop(2, slots, add_others, 0)
+    for part in (1, 0):
+        for from_far in (False, True):
+            def add_part(slot, carry):
+                for side, there, *_rest in sides:
+                    far = (far_prev, far_next)[side]
+                    when = far if from_far else jnp.logical_and(there, jnp.logical_not(far))
+                    if part in detoured:
+                        when = jnp.logical_and(when, jnp.logical_not(by_detour[side]))
+                    add_other(slot, part, side, when)
+                return carry
+
+            lax.fori_loop(2, slots, add_part, 0)
+
     if DETOURED:
         lax.fori_loop(2, slots, add_detoured, 0)
 

time: 35.5 us -> 35.5 us (level)
  no operation moved by 1% of the time
where the time goes in v6:
time: 35.5 us; the launch traced here: 35.3 us
  Pallas kernels  33.7 us (95%)
  local copies, waits for them, and re-layouts  0.97 us (3%)
  between operations  0.66 us (2%)
    pallas_call x1, Pallas kernels, on_device(): pl.pallas_call(functools.partial(kernel, n), out_shape=pltpu.VMEM(trans.s...  33.7 us
    unnamed x1, local copies, waits for them, and re-layouts  0.97 us

profile of v6, /device:TPU:96, one launch (start us, length us, event | category | flops | bytes accessed | tf_op | source)
XLA Modules:
  0.0 35.3 jit_solution(5728955959718825033)
XLA Ops:
  0.7 33.7 %windows.1 = f32[2,2,64,1024]{3,2,1,0:T(8,128)S(1)} custom-call(s32[2,4]{1,0:T(2,128)} %bitcast.1, s32[1]{0:T(128)S(6)} %copy.9.counts_hbm, f32[2,2,64,1024]{3,2,1,0:T(8,128)} %trans.1, f32[2,128,128]{2,1,0:T(8,128)} %probe_hbm.1, f32[4,128,128]{2,1,0:T(8,128)} %amp_hbm.1, bf16[4,2,256,256]{3,2,1,0:T(8,128)(2,1)} %constant.2.clone.mats_hbm), custom_call_target="tpu_custom_call" | custom-call | tf_op jit(solution)/shard_map/windows/pallas_call | solution.py:632
  34.4 1.0 %copy.8 = f32[2,2,64,1024]{3,2,1,0:T(8,128)} copy(f32[2,2,64,1024]{3,2,1,0:T(8,128)S(1)} %windows.1) | data formatting | bytes 2097152

commit v7 on v6

--- a/solution.py
+++ b/solution.py
@@ -71,17 +71,15 @@
 DETOURED = (3,)
 ALL = slice(0, HALF)
 FIRST = slice(0, EARLY)
-SECOND = slice(EARLY, 2 * EARLY)
 REST = slice(EARLY, HALF)
 
 
 def kernel(
     n, pos_hbm, counts_hbm, trans, probe_hbm, amp_hbm, mats_hbm,
     grad,
-    tile, probe, amp, mats, full_prev, full_next, more_prev, to_prev, to_next, to_partner, early_prev, early_next, early_more,
+    tile, probe, amp, mats, full_prev, full_next, to_prev, to_next, to_partner, early_prev, early_next,
     have_prev, have_next, have_own, from_prev, from_next, own, window, waves, top, bottom, passed, pos, counts, pos_prev, pos_next, pos_pass,
     here_sem, tile_sem, table_sem, pos_sem, pos_send, pos_recv, full_send, full_recv, early_send, early_recv,
-    more_send, more_recv, extra_send, extra_recv,
     part_send, part_recv, win_send, win_recv, grad_send, grad_recv, bottom_send, bottom_recv, passed_send, passed_recv, pass_send, pass_recv,
 ):
     core = lax.axis_index("depth")
@@ -153,7 +151,7 @@
                 pl.semaphore_signal(barrier, inc=1, device_id=(k, place), device_id_type=MESH)
 
     grad[...] = jnp.zeros_like(grad)
-    for padded in (tile, full_prev, full_next, more_prev):
+    for padded in (tile, full_prev, full_next):
         padded[0] = jnp.zeros(padded.shape[1:], jnp.float32)
         padded[blocks + 1] = jnp.zeros(padded.shape[1:], jnp.float32)
     for _, there, _place, where, full, have, _arrived in sides:
@@ -197,44 +195,17 @@
             full_send.at[side], full_recv.at[side], (core, place),
         )
 
-    def more_copy():
-        return remote(
-            tile.at[pl.ds(1, blocks), :, :, pl.ds(EARLY, EARLY)], more_prev.at[pl.ds(1, blocks)],
-            more_send, more_recv, (core, lat + 1),
-        )
-
-    def more_arrival():
-        return remote(
-            tile.at[pl.ds(1, blocks), :, :, pl.ds(EARLY, EARLY)], more_prev.at[pl.ds(1, blocks)],
-            more_send, more_recv, (core, lat - 1),
-        )
-
-    def when_near_or_far(side, there, far, act):
-        if side == 0:
-            pl.when(there)(functools.partial(act, EARLY))
-        else:
-            pl.when(jnp.logical_and(there, jnp.logical_not(far)))(functools.partial(act, EARLY))
-            pl.when(jnp.logical_and(there, far))(functools.partial(act, 2 * EARLY))
-
-    def win_copy(side, turn, to, place, begin):
-        slot, rows = 2 * turn + to, HALF - begin
-        return remote(
-            (to_prev, to_next)[side].at[slot, :, :, pl.ds(begin - EARLY, rows)],
-            sides[1 - side][5].at[turn, core, :, :, pl.ds(begin, rows)],
+    def win_copy(side, turn, to, place):
+        slot = 2 * turn + to
+        return remote(
+            (to_prev, to_next)[side].at[slot], sides[1 - side][5].at[turn, core, :, :, pl.ds(EARLY, HALF - EARLY)],
             win_send.at[side, slot], win_recv.at[1 - side, turn, core], (to, place),
         )
 
-    def win_arrival(side, turn, group, place, begin):
-        rows = HALF - begin
-        return remote(
-            to_prev.at[0, :, :, pl.ds(begin - EARLY, rows)], sides[side][5].at[turn, group, :, :, pl.ds(begin, rows)],
+    def win_arrival(side, turn, group, place):
+        return remote(
+            to_prev.at[0], sides[side][5].at[turn, group, :, :, pl.ds(EARLY, HALF - EARLY)],
             win_send.at[side, 0], win_recv.at[side, turn, group], (core, place),
-        )
-
-    def extra_copy(turn, group):
-        return remote(
-            early_more.at[turn], have_prev.at[turn, group, :, :, pl.ds(EARLY, EARLY)],
-            extra_send.at[turn], extra_recv.at[turn], partner,
         )
 
     def early_copy(side, turn, group):
@@ -317,10 +288,6 @@
         def _():
             full_copy(side, place).start()
 
-    @pl.when(far_next)
-    def _():
-        more_copy().start()
-
     def own_windows(turn, carry):
         have_own[turn, core] = cut(tile, pos, 2 * turn + core, ALL)
         to_partner[turn] = cut(tile, pos, 2 * turn + 1 - core, ALL)
@@ -349,10 +316,9 @@
                     (to_prev, to_next)[side][slot] = cut(tile, where, slot, REST)
 
                 for at_home, to in ((core == k, core), (core != k, 1 - core)):
-                    when_near_or_far(
-                        side, jnp.logical_and(there, at_home), far_next,
-                        lambda begin: win_copy(side, turn, to, place, begin).start(),
-                    )
+                    @pl.when(jnp.logical_and(there, at_home))
+                    def _():
+                        win_copy(side, turn, to, place).start()
 
         return carry
 
@@ -375,26 +341,14 @@
 
     lax.fori_loop(0, turns, early_windows, 0)
 
-    @pl.when(far_prev)
-    def _():
-        more_arrival().wait_recv()
-
-        def extra_windows(turn, carry):
-            have_prev[turn, core, :, :, SECOND] = cut(more_prev, pos, 2 * turn + core, FIRST)
-            early_more[turn] = cut(more_prev, pos, 2 * turn + 1 - core, FIRST)
-            extra_copy(turn, core).start()
-            return carry
-
-        lax.fori_loop(0, turns, extra_windows, 0)
-
     for load in tables_in:
         load.wait()
 
     def build_window(turn, group):
         for side, there, place, *_rest in sides:
-            when_near_or_far(
-                1 - side, there, far_prev, lambda begin: win_arrival(side, turn, group, place, begin).wait_recv()
-            )
+            @pl.when(there)
+            def _():
+                win_arrival(side, turn, group, place).wait_recv()
 
         @pl.when(core != group)
         def _():
@@ -403,10 +357,6 @@
                 @pl.when(there)
                 def _():
                     early_copy(side, turn, group).wait_recv()
-
-            @pl.when(far_prev)
-            def _():
-                extra_copy(turn, group).wait_recv()
 
         row = pos[0, 2 * turn + core] - lat * HALF
         rows = lax.broadcasted_iota(jnp.int32, (2, 2, HALF, WIN), 2)
@@ -583,10 +533,6 @@
         for copy in pos_passed_copies():
             copy.wait_send()
 
-    @pl.when(far_next)
-    def _():
-        more_copy().wait_send()
-
     def finish(turn, carry):
         part_copy(turn, core).wait_send()
         for part in range(2):
@@ -597,15 +543,8 @@
                 early_copy(side, turn, core).wait_send()
                 for layer in range(4):
                     grad_copy(side, turn, layer, core, place).wait_send()
-
-            for to in (core, 1 - core):
-                when_near_or_far(
-                    side, there, far_next, lambda begin: win_copy(side, turn, to, place, begin).wait_send()
-                )
-
-        @pl.when(far_prev)
-        def _():
-            extra_copy(turn, core).wait_send()
+                for to in (core, 1 - core):
+                    win_copy(side, turn, to, place).wait_send()
 
         return carry
 
@@ -641,11 +580,9 @@
             pltpu.VMEM(mats.shape, jnp.bfloat16),
             pltpu.VMEM((blocks + 2, 2, 2, EARLY, WIN), f32),
             pltpu.VMEM((blocks + 2, 2, 2, EARLY, WIN), f32),
-            pltpu.VMEM((blocks + 2, 2, 2, EARLY, WIN), f32),
             pltpu.VMEM((slots, 2, 2, HALF - EARLY, WIN), f32),
             pltpu.VMEM((slots, 2, 2, HALF - EARLY, WIN), f32),
             pltpu.VMEM((turns, 2, 2, HALF, WIN), f32),
-            pltpu.VMEM((turns, 2, 2, EARLY, WIN), f32),
             pltpu.VMEM((turns, 2, 2, EARLY, WIN), f32),
             pltpu.VMEM((turns, 2, 2, EARLY, WIN), f32),
             pltpu.VMEM((turns, 2, 2, 2, HALF, WIN), f32),
@@ -674,10 +611,6 @@
             sem((2,)),
             sem((2, turns)),
             sem((2, turns)),
-            sem(()),
-            sem(()),
-            sem((turns,)),
-            sem((turns,)),
             sem((turns,)),
             sem((turns,)),
             sem((2, slots)),

time: 35.5 us -> 35.4 us (level)
  no operation moved by 1% of the time
where the time goes in v7:
time: 35.4 us; the launch traced here: 35.3 us
  Pallas kernels  33.6 us (95%)
  local copies, waits for them, and re-layouts  0.97 us (3%)
  between operations  0.66 us (2%)
    pallas_call x1, Pallas kernels, on_device(): pl.pallas_call(functools.partial(kernel, n), out_shape=pltpu.VMEM(trans.s...  33.6 us
    unnamed x1, local copies, waits for them, and re-layouts  0.97 us

profile of v7, /device:TPU:96, one launch (start us, length us, event | category | flops | bytes accessed | tf_op | source)
XLA Modules:
  0.0 35.3 jit_solution(6419681765722793489)
XLA Ops:
  0.7 33.6 %windows.1 = f32[2,2,64,1024]{3,2,1,0:T(8,128)S(1)} custom-call(s32[2,4]{1,0:T(2,128)} %bitcast.1, s32[1]{0:T(128)S(6)} %copy.9.counts_hbm, f32[2,2,64,1024]{3,2,1,0:T(8,128)} %trans.1, f32[2,128,128]{2,1,0:T(8,128)} %probe_hbm.1, f32[4,128,128]{2,1,0:T(8,128)} %amp_hbm.1, bf16[4,2,256,256]{3,2,1,0:T(8,128)(2,1)} %constant.2.clone.mats_hbm), custom_call_target="tpu_custom_call" | custom-call | tf_op jit(solution)/shard_map/windows/pallas_call | solution.py:571
  34.3 1.0 %copy.8 = f32[2,2,64,1024]{3,2,1,0:T(8,128)} copy(f32[2,2,64,1024]{3,2,1,0:T(8,128)S(1)} %windows.1) | data formatting | bytes 2097152

commit v8 on v4

--- a/solution.py
+++ b/solution.py
@@ -68,7 +68,7 @@
     return jnp.where(lanes >= lane, first, second)
 
 
-DETOURED = (3, 2)
+DETOURED = (3,)
 ALL = slice(0, HALF)
 FIRST = slice(0, EARLY)
 SECOND = slice(EARLY, 2 * EARLY)
@@ -271,7 +271,7 @@
         to, place = (1 - core, lat - DETOUR) if side == 0 else (1 - core, lat + DETOUR)
         return [
             remote(
-                passed.at[part], sides[side][6].at[core, part], passed_send.at[part], grad_recv.at[side, core, part],
+                passed.at[part], sides[side][6].at[2 + core, part], passed_send.at[part], grad_recv.at[side, 2 + core, part],
                 (k, place),
             )
             for k in (core, to)
@@ -433,7 +433,7 @@
             for side, there, place, *_rest in sides:
                 goes = jnp.logical_and(there, at_home)
                 if layer in DETOURED:
-                    around = jnp.logical_and((far_prev, far_next)[side], turn == 0)
+                    around = jnp.logical_and((far_prev, far_next)[side], turn == 1)
 
                     @pl.when(jnp.logical_and(goes, around))
                     def _():
@@ -536,7 +536,7 @@
         for part in (1, 0):
             for side, there, *_rest in sides:
                 if part in detoured:
-                    there = jnp.logical_and(there, jnp.logical_not(jnp.logical_and(by_detour[side], slot < 2)))
+                    there = jnp.logical_and(there, jnp.logical_not(jnp.logical_and(by_detour[side], slot >= 2)))
                 add_other(slot, part, side, there)
         return carry
 
@@ -547,9 +547,23 @@
         return carry
 
     lax.fori_loop(0, turns, add_own, 0)
-    lax.fori_loop(0, slots, add_others, 0)
+    lax.fori_loop(0, 2, add_others, 0)
+
+    for part in (1, 0):
+        for from_far in (False, True):
+            def add_part(slot, carry):
+                for side, there, *_rest in sides:
+                    far = (far_prev, far_next)[side]
+                    when = far if from_far else jnp.logical_and(there, jnp.logical_not(far))
+                    if part in detoured:
+                        when = jnp.logical_and(when, jnp.logical_not(by_detour[side]))
+                    add_other(slot, part, side, when)
+                return carry
+
+            lax.fori_loop(2, slots, add_part, 0)
+
     if DETOURED:
-        lax.fori_loop(0, 2, add_detoured, 0)
+        lax.fori_loop(2, slots, add_detoured, 0)
 
     for side, there, place, *_rest in sides:
         @pl.when(there)

time: 36.3 us -> 35.5 us (0.978)
  Pallas kernels: 34.5 us -> 33.7 us
    pallas_call x1, Pallas kernels: 34.5 us -> 33.7 us  [on_device(): pl.pallas_call(functools.partial(kernel, n), out_shape=pltpu.VMEM(trans.s...]
where the time goes in v8:
time: 35.5 us; the launch traced here: 35.3 us
  Pallas kernels  33.7 us (95%)
  local copies, waits for them, and re-layouts  0.97 us (3%)
  between operations  0.66 us (2%)
    pallas_call x1, Pallas kernels, on_device(): pl.pallas_call(functools.partial(kernel, n), out_shape=pltpu.VMEM(trans.s...  33.7 us
    unnamed x1, local copies, waits for them, and re-layouts  0.97 us

profile of v8, /device:TPU:96, one launch (start us, length us, event | category | flops | bytes accessed | tf_op | source)
XLA Modules:
  0.0 35.3 jit_solution(2230063006178151462)
XLA Ops:
  0.7 33.7 %windows.1 = f32[2,2,64,1024]{3,2,1,0:T(8,128)S(1)} custom-call(s32[2,4]{1,0:T(2,128)} %bitcast.1, s32[1]{0:T(128)S(6)} %copy.9.counts_hbm, f32[2,2,64,1024]{3,2,1,0:T(8,128)} %trans.1, f32[2,128,128]{2,1,0:T(8,128)} %probe_hbm.1, f32[4,128,128]{2,1,0:T(8,128)} %amp_hbm.1, bf16[4,2,256,256]{3,2,1,0:T(8,128)(2,1)} %constant.2.clone.mats_hbm), custom_call_target="tpu_custom_call" | custom-call | tf_op jit(solution)/shard_map/windows/pallas_call | solution.py:632
  34.4 1.0 %copy.8 = f32[2,2,64,1024]{3,2,1,0:T(8,128)} copy(f32[2,2,64,1024]{3,2,1,0:T(8,128)S(1)} %windows.1) | data formatting | bytes 2097152
